TPU v7x, 32 devices: a whole 2x2x4 slice. The times are simulated.
32 devices in a mesh: sec: 4 (over y, x), tile: 2 (over core), lev: 4 (over z).
Axes of the slice: x: 2, y: 2, z: 4, core: 2. Of those that a mesh axis runs over, the one named last changes fastest.
Arguments:
- ocean_conc: float32 [8, 256, 512], P('lev', ('sec', 'tile')), may hold values from 0.1 to 2.9
- flow_lo: bfloat16 [256, 512], P(('sec', 'tile')), as said below
- flow_hi: bfloat16 [256, 512], P(('sec', 'tile')), as said below
- flow_y: bfloat16 [256, 512], P(('sec', 'tile')), as said below
- open_lo: int32 [256, 512], P(('sec', 'tile')), may hold values from 0 to 1, as said below
- open_hi: int32 [256, 512], P(('sec', 'tile')), may hold values from 0 to 1
- open_y: int32 [256, 512], P(('sec', 'tile')), may hold values from 0 to 1, as said below
- settle_rate: float32 [8], P('lev'), may hold values from 0.01 to 0.1
- critical_stress: float32 [8], P('lev'), may hold values from 0.05 to 0.5
- erosion_rate: float32 [8], P('lev'), may hold values from 0.002 to 0.02
- wave_energy: bfloat16 [768, 4096], P('lev', ('sec', 'tile')), may hold values from 0 to 2
- band_angle: float32 [768], P('lev'), may hold values from -3.140625 to 3.140625
- band_speed: float32 [768], P('lev'), may hold values from 0.2 to 0.3
- band_growth: float32 [768], P('lev'), may hold values from 0.05 to 0.5
- band_orbital: float32 [768], P('lev'), may hold values from 0.01 to 0.1
- neighbors: int32 [4, 4096], P(None, ('sec', 'tile')), may hold values from 0 to 4095, as said below
- facing_angle: float32 [4, 4096], P(None, ('sec', 'tile')), may hold values from -3.140625 to 3.140625
- live_nodes: int32 [4096], P(('sec', 'tile')), may hold values 0 or 1
- remap_owner: int32 [512, 1], P(('sec', 'tile')), may hold values from 0 to 7; in each aligned block of 64 rows (0 to 63, 64 to 127, ...) at most 16 rows name the same one
- remap_slot: int32 [512], P(('sec', 'tile')), may hold values from 0 to 7
- remap_cell: int32 [512], P(('sec', 'tile')), may hold values from 0 to 255
- remap_weight: bfloat16 [512, 64, 64], P(('sec', 'tile')), may hold values from -0.25 to 0.25
Outputs:
- sediment_out: float32 [8, 256, 512], P('lev', ('sec', 'tile'))
- waves_out: bfloat16 [768, 4096], P('lev', ('sec', 'tile'))
Inputs may be any that keep to these rules, and one draw needn't show every extreme that they name: open_hi of row r equals open_lo of row r + 1; the lower face of the first row and the upper face of the last row are closed. `open_y`: the face after the last column is closed. flow_lo is zero where open_lo is 0, of magnitude at most 0.150390625; flow_hi of row r equals flow_lo of row r + 1. `flow_hi`: zero where open_hi is 0, of magnitude at most 0.150390625. `flow_y`: zero where open_y is 0, of magnitude at most 0.150390625. `neighbors`: each neighbour's index differs from its node's index by at most 128. `remap_owner`: among the 64 entries of one device at most 16 name the same owner.
All inputs are finite; a program needn't handle non-finite values. No bound on the sum of `live_nodes` on one device may be relied on, other than what follows from the above.
Results may differ from a plain program's by a relative error of at most 0.001.
Values sent between devices are 32-bit elements; how exact they have to be, the bound alone decides.
A program may use at most 64 MiB of HBM per device.

v0:
```python
import jax
import jax.numpy as jnp
from jax import lax
from jax.sharding import PartitionSpec as P

OSTEPS = 4
WSTEPS = 4
NBRS = 4


KAPPA = 0.07
FORCE_SCALE = 5.0
DRAG = 50.0
TAU_CURRENT = 20.0
TAU_WAVES = 10.0
HIGHEST = lax.Precision.HIGHEST


def with_halo(x, sides, width):
    for axis, dim in sides:
        count, length = (lax.axis_size(axis), x.shape[dim])
        up = [(i, (i + 1) % count) for i in range(count - 1)]
        down = [(j, i) for i, j in up]
        last = lax.slice_in_dim(x, length - width, length, axis=dim)
        first = lax.slice_in_dim(x, 0, width, axis=dim)
        before = lax.ppermute(last, axis, up)
        after = lax.ppermute(first, axis, down)
        x = jnp.concatenate([before, x, after], axis=dim)
    return x


def coupling_fields(flow_lo, flow_hi, flow_y):
    eastward = 0.5 * (flow_lo.astype(jnp.float32) + flow_hi.astype(jnp.float32))
    across = flow_y.astype(jnp.float32)
    earlier = jnp.pad(across, ((0, 0), (1, 0)))[:, :-1]
    northward = 0.5 * (across + earlier)
    current_speed = jnp.sqrt(eastward * eastward + northward * northward)
    forcing = jnp.stack(
        [
            FORCE_SCALE * eastward,
            FORCE_SCALE * northward,
            DRAG * current_speed * eastward,
            DRAG * current_speed * northward,
        ]
    )
    return (forcing, eastward * eastward + northward * northward)


def band_rates(wave_forcing, band_dir, band_pace, growth, facing):
    cosines = jnp.cos(band_dir)[:, None]
    sine_terms = jnp.sin(band_dir)[:, None]
    drift_term = cosines * wave_forcing[0][None, :] + sine_terms * wave_forcing[1][None, :]
    push_term = jnp.maximum(
        cosines * wave_forcing[2][None, :] + sine_terms * wave_forcing[3][None, :], 0.0
    )
    base_rate = 0.5 * band_pace[:, None] * (1.0 + 0.5 * jnp.tanh(drift_term))
    inflow = base_rate[None] * jnp.maximum(
        -jnp.cos(band_dir[None, :, None] - facing[:, None, :]), 0.0
    )
    return (growth[:, None] * push_term, inflow)


def ocean_step(
    sediment,
    above_rows,
    below_rows,
    flow_lo,
    flow_hi,
    flow_y,
    open_lo,
    open_hi,
    open_y,
    settle_rate,
    erosion_gain,
):
    right_cells = jnp.pad(sediment, ((0, 0), (0, 0), (0, 1)))[:, :, 1:]
    flux_lo = (
        jnp.maximum(flow_lo, 0.0) * above_rows
        + jnp.minimum(flow_lo, 0.0) * sediment
        - KAPPA * open_lo * (sediment - above_rows)
    )
    flux_hi = (
        jnp.maximum(flow_hi, 0.0) * sediment
        + jnp.minimum(flow_hi, 0.0) * below_rows
        - KAPPA * open_hi * (below_rows - sediment)
    )
    flux_y = (
        jnp.maximum(flow_y, 0.0) * sediment
        + jnp.minimum(flow_y, 0.0) * right_cells
        - KAPPA * open_y * (right_cells - sediment)
    )
    flux_left = jnp.pad(flux_y, ((0, 0), (0, 0), (1, 0)))[:, :, :-1]
    return (
        sediment
        - (flux_hi - flux_lo)
        - (flux_y - flux_left)
        - settle_rate[:, None, None] * sediment
        + erosion_gain
    )


def entry_rank(owners, peer_count):
    onehot = (owners[:, None] == jnp.arange(peer_count, dtype=jnp.int32)[None, :]).astype(jnp.int32)
    earlier = jnp.cumsum(onehot, axis=0) - onehot
    return jnp.sum(earlier * onehot, axis=1)


def per_device(
    ocean_conc,
    flow_lo,
    flow_hi,
    flow_y,
    open_lo,
    open_hi,
    open_y,
    settle_rate,
    critical_stress,
    erosion_rate,
    wave_energy,
    band_angle,
    band_speed,
    band_growth,
    band_orbital,
    neighbors,
    facing_angle,
    live_nodes,
    remap_owner,
    remap_slot,
    remap_cell,
    remap_weight,
):
    peer_count = lax.axis_size(("sec", "tile"))
    entry_count = remap_cell.shape[0]
    capacity = min(entry_count, max(2, 2 * entry_count // peer_count))
    slot_count = peer_count * capacity
    row_count, column_count = flow_lo.shape
    ocean_count = row_count * column_count // 64
    node_count = wave_energy.shape[1]
    block_count = node_count // 64
    forcing, current_square = coupling_fields(flow_lo, flow_hi, flow_y)
    weights = remap_weight.astype(jnp.float32)
    picked = jnp.transpose(forcing.reshape(4, ocean_count, 64)[:, remap_cell, :], (1, 0, 2))
    pieces = jnp.einsum("eji,eci->ecj", weights, picked, precision=HIGHEST).reshape(
        entry_count, 256
    )
    owners = remap_owner[:, 0]
    ranking = entry_rank(owners, peer_count)
    position = owners * capacity + ranking
    send_rows = jnp.zeros((slot_count, 256), jnp.float32).at[position].set(pieces)
    send_ids = jnp.full((slot_count,), -1, jnp.int32).at[position].set(remap_slot)
    got_rows, got_ids = (
        lax.all_to_all(send_rows, ("sec", "tile"), split_axis=0, concat_axis=0, tiled=True),
        lax.all_to_all(send_ids, ("sec", "tile"), split_axis=0, concat_axis=0, tiled=True),
    )
    block_index = jnp.arange(block_count, dtype=jnp.int32)
    select = (got_ids[None, :] == block_index[:, None]).astype(jnp.float32)
    wave_blocks = jnp.dot(select, got_rows, precision=HIGHEST)
    wave_forcing = jnp.transpose(wave_blocks.reshape(block_count, 4, 64), (1, 0, 2)).reshape(
        4, node_count
    )
    alive_mask = live_nodes.astype(jnp.float32)[None, :]
    source_term, inflow = band_rates(
        wave_forcing, band_angle, band_speed, band_growth, facing_angle
    )
    energy = (wave_energy.astype(jnp.float32) + source_term) * alive_mask
    first_node = lax.axis_index(("sec", "tile")) * node_count
    total_rate = jnp.sum(inflow, axis=0)
    local_index = neighbors - first_node + 128
    for sweep in range(WSTEPS):
        padded = with_halo(energy, ((("sec", "tile"), 1),), 128)
        arriving = jnp.zeros_like(energy)
        for neighbor in range(NBRS):
            arriving = arriving + inflow[neighbor] * jnp.take(padded, local_index[neighbor], axis=1)
        energy = (energy + arriving - total_rate * energy) * alive_mask
    waves_out = energy.astype(jnp.bfloat16)
    coefficient = jnp.stack(
        [band_orbital * jnp.cos(band_angle), band_orbital * jnp.sin(band_angle)]
    )
    orbital = lax.psum(jnp.dot(coefficient, energy, precision=HIGHEST), "lev")
    orbital_blocks = jnp.transpose(orbital.reshape(2, block_count, 64), (1, 0, 2)).reshape(
        block_count, 128
    )
    back_rows = jnp.einsum("ws,wc->sc", select, orbital_blocks, precision=HIGHEST)
    returned = lax.all_to_all(back_rows, ("sec", "tile"), split_axis=0, concat_axis=0, tiled=True)
    mine = returned[position].reshape(entry_count, 2, 64)
    spread = jnp.einsum("eji,ecj->eci", weights, mine, precision=HIGHEST).reshape(entry_count, 128)
    ocean_select = (
        remap_cell[None, :] == jnp.arange(ocean_count, dtype=jnp.int32)[:, None]
    ).astype(jnp.float32)
    ocean_blocks = jnp.dot(ocean_select, spread, precision=HIGHEST)
    ocean_orbital = jnp.transpose(ocean_blocks.reshape(ocean_count, 2, 64), (1, 0, 2)).reshape(
        2, row_count, column_count
    )
    stress = TAU_CURRENT * current_square + TAU_WAVES * (
        ocean_orbital[0] * ocean_orbital[0] + ocean_orbital[1] * ocean_orbital[1]
    )
    erosion_gain = erosion_rate[:, None, None] * jnp.maximum(
        stress[None] / critical_stress[:, None, None] - 1.0, 0.0
    )
    lower_flow = flow_lo.astype(jnp.float32)
    upper_flow = flow_hi.astype(jnp.float32)
    side_flow = flow_y.astype(jnp.float32)
    lower_open = open_lo.astype(jnp.float32)
    upper_open = open_hi.astype(jnp.float32)
    side_open = open_y.astype(jnp.float32)
    sediment = ocean_conc
    for sweep in range(OSTEPS):
        rimmed = with_halo(sediment, ((("sec", "tile"), 1),), 1)
        sediment = ocean_step(
            sediment,
            rimmed[:, :-2],
            rimmed[:, 2:],
            lower_flow,
            upper_flow,
            side_flow,
            lower_open,
            upper_open,
            side_open,
            settle_rate,
            erosion_gain,
        )
    return (sediment, waves_out)


def solution(mesh):
    return jax.shard_map(
        per_device,
        mesh=mesh,
        in_specs=(
            P("lev", ("sec", "tile"), None),
            P(("sec", "tile"), None),
            P(("sec", "tile"), None),
            P(("sec", "tile"), None),
            P(("sec", "tile"), None),
            P(("sec", "tile"), None),
            P(("sec", "tile"), None),
            P("lev"),
            P("lev"),
            P("lev"),
            P("lev", ("sec", "tile")),
            P("lev"),
            P("lev"),
            P("lev"),
            P("lev"),
            P(None, ("sec", "tile")),
            P(None, ("sec", "tile")),
            P(("sec", "tile")),
            P(("sec", "tile"), None),
            P(("sec", "tile")),
            P(("sec", "tile")),
            P(("sec", "tile"), None, None),
        ),
        out_specs=(P("lev", ("sec", "tile"), None), P("lev", ("sec", "tile"))),
        check_vma=False,
    )
```

profile of v0, /device:TPU:3, one launch (start us, length us, event | category | flops | bytes accessed | tf_op | source)
XLA Modules:
  0.0 172.4 jit_solution(4491737186999810941)
XLA Ops:
  4.7 4.6 %all-to-all-start = ((s32[8,16,1]{1,2,0:T(1,128)}), s32[8,16,1]{1,2,0:T(1,128)S(1)}, u32[]{:S(2)}, u32[]{:S(2)}) async-start(s32[8,16,1]{1,2,0:T(1,128)} %bitcast.4), calls=%async_computation | async-start | bytes 8192 | tf_op jit(solution)/shard_map/all_to_all | solution.py:153
  10.6 2.3 %collective-permute-start = (f32[2,1,512]{2,1,0:T(1,128)}, f32[2,1,512]{2,1,0:T(1,128)}, u32[]{:S(2)}, u32[]{:S(2)}) collective-permute-start(f32[2,1,512]{2,1,0:T(1,128)} %get-tuple-element.31), channel_id=1, source_target_pairs={{4,0},{8,4},{12,8},{16,12},{20,16},{24,20},{28,24},{5,1},{9,5},{13... | collective-permute-start | bytes 12296 | tf_op jit(solution)/shard_map/ppermute | solution.py:27
  12.9 4.2 %collective-permute-start.1 = (f32[2,1,512]{2,1,0:T(1,128)}, f32[2,1,512]{2,1,0:T(1,128)}, u32[]{:S(2)}, u32[]{:S(2)}) collective-permute-start(f32[2,1,512]{2,1,0:T(1,128)} %get-tuple-element.32), channel_id=1, source_target_pairs={{0,4},{4,8},{8,12},{12,16},{16,20},{20,24},{24,28},{1,5},{5,9},{9,... | collective-permute-start | bytes 12296 | tf_op jit(solution)/shard_map/ppermute | solution.py:26
  20.4 1.5 fusion.100
  25.2 1.7 fusion.134
  28.6 3.3 %all-to-all-start.1 = ((f32[8,16,256]{2,1,0:T(8,128)}), f32[8,16,256]{2,1,0:T(8,128)S(1)}, u32[]{:S(2)}, u32[]{:S(2)}) async-start(f32[8,16,256]{2,1,0:T(8,128)} %bitcast.14), calls=%async_computation.1 | async-start | bytes 262144 | tf_op jit(solution)/shard_map/all_to_all | solution.py:152
  33.5 1.8 %all-to-all-done.1 = f32[8,16,256]{2,1,0:T(8,128)S(1)} async-done(((f32[8,16,256]{2,1,0:T(8,128)}), f32[8,16,256]{2,1,0:T(8,128)S(1)}, u32[]{:S(2)}, u32[]{:S(2)}) %all-to-all-start.1) | async-done | bytes 131104 | tf_op jit(solution)/shard_map/all_to_all | solution.py:152
  36.4 4.0 %collective-permute-start.2 = (f32[192,128]{0,1:T(8,128)S(1)}, f32[192,128]{0,1:T(8,128)S(1)}, u32[]{:S(2)}, u32[]{:S(2)}) collective-permute-start(f32[192,128]{0,1:T(8,128)S(1)} %get-tuple-element.21), channel_id=1, source_target_pairs={{0,4},{4,8},{8,12},{12,16},{16,20},{20,24},{24,28},{1,5},{5,9},{9,... | collective-permute-start | bytes 294920 | tf_op jit(solution)/shard_map/ppermute | solution.py:26
  40.4 1.9 %collective-permute-start.3 = (f32[192,128]{0,1:T(8,128)S(1)}, f32[192,128]{0,1:T(8,128)S(1)}, u32[]{:S(2)}, u32[]{:S(2)}) collective-permute-start(f32[192,128]{0,1:T(8,128)S(1)} %get-tuple-element.22), channel_id=1, source_target_pairs={{4,0},{8,4},{12,8},{16,12},{20,16},{24,20},{28,24},{5,1},{9,5},{13... | collective-permute-start | bytes 294920 | tf_op jit(solution)/shard_map/ppermute | solution.py:27
  42.4 8.5 %maximum_multiply_fusion = (f32[4,192,512]{1,2,0:T(8,128)}, f32[192,512]{0,1:T(8,128)S(1)}) fusion(f32[4,512]{1,0:T(4,128)S(1)} %copy-done.38, f32[192]{0:T(256)S(1)} %copy-done.43, f32[192,512]{0,1:T(8,128)S(1)} %get-tuple-element.49), kind=kLoop, calls=%fused_computation.20 | loop fusion | flops 1867776 | bytes 2368256 | tf_op jit(solution)/shard_map/mul | solution.py:57
  50.9 2.2 %gather_fusion.2 = f32[512,192]{1,0:T(8,128)} fusion(f32[192,768]{0,1:T(8,128)S(1)} %pad_maximum_fusion, s32[1024]{0:T(1024)S(1)} %pad_clamp_fusion.4), kind=kCustom, calls=%fused_computation.clone | custom fusion | bytes 788480 | tf_op jit(solution)/shard_map/jit(_take)/gather | solution.py:173
  53.2 2.2 %gather_fusion.3 = f32[512,192]{1,0:T(8,128)} fusion(f32[192,768]{0,1:T(8,128)S(1)} %pad_maximum_fusion, s32[1024]{0:T(1024)S(1)} %pad_clamp_fusion.3), kind=kCustom, calls=%fused_computation.1.clone | custom fusion | bytes 788480 | tf_op jit(solution)/shard_map/jit(_take)/gather | solution.py:173
  55.4 2.2 %gather_fusion.4 = f32[512,192]{1,0:T(8,128)} fusion(f32[192,768]{0,1:T(8,128)S(1)} %pad_maximum_fusion, s32[1024]{0:T(1024)S(1)} %pad_clamp_fusion.2), kind=kCustom, calls=%fused_computation.2.clone | custom fusion | bytes 788480 | tf_op jit(solution)/shard_map/jit(_take)/gather | solution.py:173
  57.6 2.2 %gather_fusion.5 = f32[512,192]{1,0:T(8,128)} fusion(f32[192,768]{0,1:T(8,128)S(1)} %pad_maximum_fusion, s32[1024]{0:T(1024)S(1)} %pad_clamp_fusion.1), kind=kCustom, calls=%fused_computation.3.clone | custom fusion | bytes 788480 | tf_op jit(solution)/shard_map/jit(_take)/gather | solution.py:173
  59.9 2.6 %fusion.21 = f32[192,512]{0,1:T(8,128)S(1)} fusion(f32[512,192]{1,0:T(8,128)} %gather_fusion.5, f32[512,192]{1,0:T(8,128)} %gather_fusion.4, f32[512,192]{1,0:T(8,128)} %gather_fusion.3, f32[512,192]{1,0:T(8,128)} %gather_fusion.2, f32[192,512]{0,1:T(8,128)S(1)} %get-tuple-element.14, f32[4,192,512]{1,2,0:T(8,128)} %get-tuple-element.13, ...), kind=kLoop, calls=%fused_computation.66 | loop fusion | flops 2260992 | bytes 4139264 | tf_op jit(solution)/shard_map/mul | solution.py:174
  62.6 4.5 %collective-permute-start.4 = (f32[192,128]{0,1:T(8,128)S(1)}, f32[192,128]{0,1:T(8,128)S(1)}, u32[]{:S(2)}, u32[]{:S(2)}) collective-permute-start(f32[192,128]{0,1:T(8,128)S(1)} %get-tuple-element.19), channel_id=1, source_target_pairs={{0,4},{4,8},{8,12},{12,16},{16,20},{20,24},{24,28},{1,5},{5,9},{9,... | collective-permute-start | bytes 294920 | tf_op jit(solution)/shard_map/ppermute | solution.py:26
  67.1 1.9 %collective-permute-start.5 = (f32[192,128]{0,1:T(8,128)S(1)}, f32[192,128]{0,1:T(8,128)S(1)}, u32[]{:S(2)}, u32[]{:S(2)}) collective-permute-start(f32[192,128]{0,1:T(8,128)S(1)} %get-tuple-element.20), channel_id=1, source_target_pairs={{4,0},{8,4},{12,8},{16,12},{20,16},{24,20},{28,24},{5,1},{9,5},{13... | collective-permute-start | bytes 294920 | tf_op jit(solution)/shard_map/ppermute | solution.py:27
  69.9 4.5 %collective-permute-done.5 = f32[192,128]{0,1:T(8,128)S(1)} collective-permute-done((f32[192,128]{0,1:T(8,128)S(1)}, f32[192,128]{0,1:T(8,128)S(1)}, u32[]{:S(2)}, u32[]{:S(2)}) %collective-permute-start.5) | collective-permute-done | bytes 98336 | tf_op jit(solution)/shard_map/ppermute | solution.py:27
  74.4 2.2 %gather_fusion.6 = f32[512,192]{1,0:T(8,128)} fusion(f32[192,768]{0,1:T(8,128)S(1)} %pad_maximum_fusion.1, s32[1024]{0:T(1024)S(1)} %pad_clamp_fusion.4), kind=kCustom, calls=%fused_computation.4.clone | custom fusion | bytes 788480 | tf_op jit(solution)/shard_map/jit(_take)/gather | solution.py:173
  76.6 2.2 %gather_fusion.7 = f32[512,192]{1,0:T(8,128)} fusion(f32[192,768]{0,1:T(8,128)S(1)} %pad_maximum_fusion.1, s32[1024]{0:T(1024)S(1)} %pad_clamp_fusion.3), kind=kCustom, calls=%fused_computation.5.clone | custom fusion | bytes 788480 | tf_op jit(solution)/shard_map/jit(_take)/gather | solution.py:173
  78.8 2.2 %gather_fusion.8 = f32[512,192]{1,0:T(8,128)} fusion(f32[192,768]{0,1:T(8,128)S(1)} %pad_maximum_fusion.1, s32[1024]{0:T(1024)S(1)} %pad_clamp_fusion.2), kind=kCustom, calls=%fused_computation.6.clone | custom fusion | bytes 788480 | tf_op jit(solution)/shard_map/jit(_take)/gather | solution.py:173
  81.0 2.2 %gather_fusion.9 = f32[512,192]{1,0:T(8,128)} fusion(f32[192,768]{0,1:T(8,128)S(1)} %pad_maximum_fusion.1, s32[1024]{0:T(1024)S(1)} %pad_clamp_fusion.1), kind=kCustom, calls=%fused_computation.7.clone | custom fusion | bytes 788480 | tf_op jit(solution)/shard_map/jit(_take)/gather | solution.py:173
  83.3 2.6 %fusion.15 = f32[192,512]{0,1:T(8,128)S(1)} fusion(f32[192,512]{0,1:T(8,128)S(1)} %fusion.21, f32[512,192]{1,0:T(8,128)} %gather_fusion.9, f32[512,192]{1,0:T(8,128)} %gather_fusion.8, f32[512,192]{1,0:T(8,128)} %gather_fusion.7, f32[512,192]{1,0:T(8,128)} %gather_fusion.6, f32[192,512]{0,1:T(8,128)S(1)} %get-tuple-element.14, ...), kind=kLoop, calls=%fused_computation.56 | loop fusion | flops 1474560 | bytes 4329472 | tf_op jit(solution)/shard_map/mul | solution.py:174
  85.9 1.9 %collective-permute-start.6 = (f32[192,128]{0,1:T(8,128)S(1)}, f32[192,128]{0,1:T(8,128)S(1)}, u32[]{:S(2)}, u32[]{:S(2)}) collective-permute-start(f32[192,128]{0,1:T(8,128)S(1)} %get-tuple-element.17), channel_id=1, source_target_pairs={{0,4},{4,8},{8,12},{12,16},{16,20},{20,24},{24,28},{1,5},{5,9},{9,... | collective-permute-start | bytes 294920 | tf_op jit(solution)/shard_map/ppermute | solution.py:26
  87.8 2.6 %collective-permute-start.7 = (f32[192,128]{0,1:T(8,128)S(1)}, f32[192,128]{0,1:T(8,128)S(1)}, u32[]{:S(2)}, u32[]{:S(2)}) collective-permute-start(f32[192,128]{0,1:T(8,128)S(1)} %get-tuple-element.18), channel_id=1, source_target_pairs={{4,0},{8,4},{12,8},{16,12},{20,16},{24,20},{28,24},{5,1},{9,5},{13... | collective-permute-start | bytes 294920 | tf_op jit(solution)/shard_map/ppermute | solution.py:27
  91.1 3.9 %collective-permute-done.7 = f32[192,128]{0,1:T(8,128)S(1)} collective-permute-done((f32[192,128]{0,1:T(8,128)S(1)}, f32[192,128]{0,1:T(8,128)S(1)}, u32[]{:S(2)}, u32[]{:S(2)}) %collective-permute-start.7) | collective-permute-done | bytes 98336 | tf_op jit(solution)/shard_map/ppermute | solution.py:27
  95.0 2.2 %gather_fusion.10 = f32[512,192]{1,0:T(8,128)} fusion(f32[192,768]{0,1:T(8,128)S(1)} %pad_maximum_fusion.2, s32[1024]{0:T(1024)S(1)} %pad_clamp_fusion.4), kind=kCustom, calls=%fused_computation.8.clone | custom fusion | bytes 788480 | tf_op jit(solution)/shard_map/jit(_take)/gather | solution.py:173
  97.3 2.2 %gather_fusion.11 = f32[512,192]{1,0:T(8,128)} fusion(f32[192,768]{0,1:T(8,128)S(1)} %pad_maximum_fusion.2, s32[1024]{0:T(1024)S(1)} %pad_clamp_fusion.3), kind=kCustom, calls=%fused_computation.9.clone | custom fusion | bytes 788480 | tf_op jit(solution)/shard_map/jit(_take)/gather | solution.py:173
  99.5 2.2 %gather_fusion.12 = f32[512,192]{1,0:T(8,128)} fusion(f32[192,768]{0,1:T(8,128)S(1)} %pad_maximum_fusion.2, s32[1024]{0:T(1024)S(1)} %pad_clamp_fusion.2), kind=kCustom, calls=%fused_computation.10.clone | custom fusion | bytes 788480 | tf_op jit(solution)/shard_map/jit(_take)/gather | solution.py:173
  101.7 2.2 %gather_fusion.13 = f32[512,192]{1,0:T(8,128)} fusion(f32[192,768]{0,1:T(8,128)S(1)} %pad_maximum_fusion.2, s32[1024]{0:T(1024)S(1)} %copy-done.22), kind=kCustom, calls=%fused_computation.11.clone | custom fusion | bytes 788480 | tf_op jit(solution)/shard_map/jit(_take)/gather | solution.py:173
  104.0 2.6 %fusion.9 = f32[192,512]{0,1:T(8,128)S(1)} fusion(f32[192,512]{0,1:T(8,128)S(1)} %fusion.15, f32[512,192]{1,0:T(8,128)} %gather_fusion.13, f32[512,192]{1,0:T(8,128)} %gather_fusion.12, f32[512,192]{1,0:T(8,128)} %gather_fusion.11, f32[512,192]{1,0:T(8,128)} %gather_fusion.10, f32[192,512]{0,1:T(8,128)S(1)} %get-tuple-element.14, ...), kind=kLoop, calls=%fused_computation.46 | loop fusion | flops 1474560 | bytes 4329472 | tf_op jit(solution)/shard_map/mul | solution.py:174
  106.5 1.9 %collective-permute-start.8 = (f32[192,128]{0,1:T(8,128)S(1)}, f32[192,128]{0,1:T(8,128)S(1)}, u32[]{:S(2)}, u32[]{:S(2)}) collective-permute-start(f32[192,128]{0,1:T(8,128)S(1)} %get-tuple-element.15), channel_id=1, source_target_pairs={{0,4},{4,8},{8,12},{12,16},{16,20},{20,24},{24,28},{1,5},{5,9},{9,... | collective-permute-start | bytes 294920 | tf_op jit(solution)/shard_map/ppermute | solution.py:26
  108.5 2.4 %collective-permute-start.9 = (f32[192,128]{0,1:T(8,128)S(1)}, f32[192,128]{0,1:T(8,128)S(1)}, u32[]{:S(2)}, u32[]{:S(2)}) collective-permute-start(f32[192,128]{0,1:T(8,128)S(1)} %get-tuple-element.16), channel_id=1, source_target_pairs={{4,0},{8,4},{12,8},{16,12},{20,16},{24,20},{28,24},{5,1},{9,5},{13... | collective-permute-start | bytes 294920 | tf_op jit(solution)/shard_map/ppermute | solution.py:27
  111.5 4.2 %collective-permute-done.9 = f32[192,128]{0,1:T(8,128)S(1)} collective-permute-done((f32[192,128]{0,1:T(8,128)S(1)}, f32[192,128]{0,1:T(8,128)S(1)}, u32[]{:S(2)}, u32[]{:S(2)}) %collective-permute-start.9) | collective-permute-done | bytes 98336 | tf_op jit(solution)/shard_map/ppermute | solution.py:27
  115.7 1.6 gather_fusion.14
  117.3 2.2 %gather_fusion.15 = f32[512,192]{1,0:T(8,128)} fusion(f32[192,768]{0,1:T(8,128)S(1)} %pad_maximum_fusion.3, s32[1024]{0:T(1024)S(1)} %pad_clamp_fusion.3), kind=kCustom, calls=%fused_computation.13.clone | custom fusion | bytes 788480 | tf_op jit(solution)/shard_map/jit(_take)/gather | solution.py:173
  119.5 2.2 %gather_fusion.16 = f32[512,192]{1,0:T(8,128)} fusion(f32[192,768]{0,1:T(8,128)S(1)} %pad_maximum_fusion.3, s32[1024]{0:T(1024)S(1)} %pad_clamp_fusion.2), kind=kCustom, calls=%fused_computation.14.clone | custom fusion | bytes 788480 | tf_op jit(solution)/shard_map/jit(_take)/gather | solution.py:173
  121.8 2.2 %gather_fusion.17 = f32[512,192]{1,0:T(8,128)} fusion(f32[192,768]{0,1:T(8,128)S(1)} %pad_maximum_fusion.3, s32[1024]{0:T(1024)S(1)} %copy-done.23), kind=kCustom, calls=%fused_computation.15.clone | custom fusion | bytes 788480 | tf_op jit(solution)/shard_map/jit(_take)/gather | solution.py:173
  124.0 2.4 %fusion.119 = (bf16[192,512]{0,1:T(8,128)(2,1)S(1)}, f32[192,512]{0,1:T(8,128)S(1)}) fusion(f32[512]{0:T(512)S(1)} %convert_element_type.56, f32[192,512]{0,1:T(8,128)S(1)} %get-tuple-element.14, f32[192,512]{0,1:T(8,128)S(1)} %fusion.9, f32[512,192]{1,0:T(8,128)} %gather_fusion.17, pred[512]{0:T(512)(128)(4,1)S(1)} %copy-done.33, ...), kind=kLoop, calls=%fused_computation.229 | loop fusion | flops 1572864 | bytes 4526080 | tf_op jit(solution)/shard_map/convert_element_type | solution.py:175
  127.3 9.9 %psum.7 = f32[8,128]{1,0:T(8,128)S(1)} all-reduce(f32[8,128]{1,0:T(8,128)S(1)} %reshape.175), channel_id=1, replica_groups=mesh['sec'=4,'tile'=2,'lev'=4] {'lev'}, use_global_device_ids=true, to_apply=%region_5.7 | all-reduce | flops 1024 | bytes 8192 | tf_op jit(solution)/shard_map/psum | solution.py:179
  138.1 3.8 %all-to-all-start.2 = ((f32[8,16,128]{2,1,0:T(8,128)}), f32[8,16,128]{2,1,0:T(8,128)S(1)}, u32[]{:S(2)}, u32[]{:S(2)}) async-start(f32[8,16,128]{2,1,0:T(8,128)} %fusion.104), calls=%async_computation.2 | async-start | bytes 131072 | tf_op jit(solution)/shard_map/all_to_all | solution.py:184
  143.4 1.9 %all-to-all-done.2 = f32[8,16,128]{2,1,0:T(8,128)S(1)} async-done(((f32[8,16,128]{2,1,0:T(8,128)}), f32[8,16,128]{2,1,0:T(8,128)S(1)}, u32[]{:S(2)}, u32[]{:S(2)}) %all-to-all-start.2) | async-done | bytes 65568 | tf_op jit(solution)/shard_map/all_to_all | solution.py:184
  148.6 2.5 %collective-permute-start.10 = (f32[2,1,512]{2,1,0:T(1,128)S(1)}, f32[2,1,512]{2,1,0:T(1,128)S(1)}, u32[]{:S(2)}, u32[]{:S(2)}) collective-permute-start(f32[2,1,512]{2,1,0:T(1,128)S(1)} %get-tuple-element.27), channel_id=1, source_target_pairs={{4,0},{8,4},{12,8},{16,12},{20,16},{24,20},{28,24},{5,1},{9,5},{13... | collective-permute-start | bytes 12296 | tf_op jit(solution)/shard_map/ppermute | solution.py:27
  151.1 4.0 %collective-permute-start.11 = (f32[2,1,512]{2,1,0:T(1,128)S(1)}, f32[2,1,512]{2,1,0:T(1,128)S(1)}, u32[]{:S(2)}, u32[]{:S(2)}) collective-permute-start(f32[2,1,512]{2,1,0:T(1,128)S(1)} %get-tuple-element.28), channel_id=1, source_target_pairs={{0,4},{4,8},{8,12},{12,16},{16,20},{20,24},{24,28},{1,5},{5,9},{9,... | collective-permute-start | bytes 12296 | tf_op jit(solution)/shard_map/ppermute | solution.py:26
  155.9 2.8 %collective-permute-start.12 = (f32[2,1,512]{2,1,0:T(1,128)S(1)}, f32[2,1,512]{2,1,0:T(1,128)S(1)}, u32[]{:S(2)}, u32[]{:S(2)}) collective-permute-start(f32[2,1,512]{2,1,0:T(1,128)S(1)} %get-tuple-element.25), channel_id=1, source_target_pairs={{4,0},{8,4},{12,8},{16,12},{20,16},{24,20},{28,24},{5,1},{9,5},{13... | collective-permute-start | bytes 12296 | tf_op jit(solution)/shard_map/ppermute | solution.py:27
  158.8 4.2 %collective-permute-start.13 = (f32[2,1,512]{2,1,0:T(1,128)S(1)}, f32[2,1,512]{2,1,0:T(1,128)S(1)}, u32[]{:S(2)}, u32[]{:S(2)}) collective-permute-start(f32[2,1,512]{2,1,0:T(1,128)S(1)} %get-tuple-element.26), channel_id=1, source_target_pairs={{0,4},{4,8},{8,12},{12,16},{16,20},{20,24},{24,28},{1,5},{5,9},{9,... | collective-permute-start | bytes 12296 | tf_op jit(solution)/shard_map/ppermute | solution.py:26
  163.9 1.9 %collective-permute-start.14 = (f32[2,1,512]{2,1,0:T(1,128)S(1)}, f32[2,1,512]{2,1,0:T(1,128)S(1)}, u32[]{:S(2)}, u32[]{:S(2)}) collective-permute-start(f32[2,1,512]{2,1,0:T(1,128)S(1)} %get-tuple-element.23), channel_id=1, source_target_pairs={{4,0},{8,4},{12,8},{16,12},{20,16},{24,20},{28,24},{5,1},{9,5},{13... | collective-permute-start | bytes 12296 | tf_op jit(solution)/shard_map/ppermute | solution.py:27
  165.8 5.1 %collective-permute-start.15 = (f32[2,1,512]{2,1,0:T(1,128)S(1)}, f32[2,1,512]{2,1,0:T(1,128)S(1)}, u32[]{:S(2)}, u32[]{:S(2)}) collective-permute-start(f32[2,1,512]{2,1,0:T(1,128)S(1)} %get-tuple-element.24), channel_id=1, source_target_pairs={{0,4},{4,8},{8,12},{12,16},{16,20},{20,24},{24,28},{1,5},{5,9},{9,... | collective-permute-start | bytes 12296 | tf_op jit(solution)/shard_map/ppermute | solution.py:26
  (204 shorter events, 28.0 us)
Async XLA Ops:
  0.6 24.5 %copy-start = (bf16[64,64,64]{2,1,0:T(8,128)(2,1)S(1)}, bf16[64,64,64]{2,1,0:T(8,128)(2,1)}, u32[]{:S(2)}) copy-start(bf16[64,64,64]{2,1,0:T(8,128)(2,1)} %param.45) | copy-start | bytes 1572868
  3.1 24.1 %copy-start.52 = (s32[64]{0:T(128)}, s32[64]{0:T(128)S(1)}, u32[]{:S(2)}) copy-start(s32[64]{0:T(128)S(1)} %fusion.115) | copy-start | bytes 772
  4.7 23.9 %all-to-all-start = ((s32[8,16,1]{1,2,0:T(1,128)}), s32[8,16,1]{1,2,0:T(1,128)S(1)}, u32[]{:S(2)}, u32[]{:S(2)}) async-start(s32[8,16,1]{1,2,0:T(1,128)} %bitcast.4), calls=%async_computation | async-start | bytes 8192 | tf_op jit(solution)/shard_map/all_to_all | solution.py:153
  10.6 137.0 %collective-permute-start = (f32[2,1,512]{2,1,0:T(1,128)}, f32[2,1,512]{2,1,0:T(1,128)}, u32[]{:S(2)}, u32[]{:S(2)}) collective-permute-start(f32[2,1,512]{2,1,0:T(1,128)} %get-tuple-element.31), channel_id=1, source_target_pairs={{4,0},{8,4},{12,8},{16,12},{20,16},{24,20},{28,24},{5,1},{9,5},{13... | collective-permute-start | bytes 12296 | tf_op jit(solution)/shard_map/ppermute | solution.py:27
  12.9 134.8 %collective-permute-start.1 = (f32[2,1,512]{2,1,0:T(1,128)}, f32[2,1,512]{2,1,0:T(1,128)}, u32[]{:S(2)}, u32[]{:S(2)}) collective-permute-start(f32[2,1,512]{2,1,0:T(1,128)} %get-tuple-element.32), channel_id=1, source_target_pairs={{0,4},{4,8},{8,12},{12,16},{16,20},{20,24},{24,28},{1,5},{5,9},{9,... | collective-permute-start | bytes 12296 | tf_op jit(solution)/shard_map/ppermute | solution.py:26
  23.9 45.2 %copy-start.3 = (f32[32,512]{1,0:T(8,128)}, f32[32,512]{1,0:T(8,128)S(1)}, u32[]{:S(2)}) copy-start(f32[32,512]{1,0:T(8,128)S(1)} %get-tuple-element.38) | copy-start | bytes 196612
  23.9 45.2 %copy-start.5 = (f32[32,512]{1,0:T(8,128)}, f32[32,512]{1,0:T(8,128)S(1)}, u32[]{:S(2)}) copy-start(f32[32,512]{1,0:T(8,128)S(1)} %get-tuple-element.39) | copy-start | bytes 196612
  23.9 45.2 %copy-start.7 = (f32[32,512]{1,0:T(8,128)}, f32[32,512]{1,0:T(8,128)S(1)}, u32[]{:S(2)}) copy-start(f32[32,512]{1,0:T(8,128)S(1)} %get-tuple-element.54) | copy-start | bytes 196612
  23.9 12.1 %copy-start.46 = (f32[192]{0:T(256)S(1)}, f32[192]{0:T(256)}, u32[]{:S(2)}) copy-start(f32[192]{0:T(256)} %param.37) | copy-start | bytes 2308
  25.2 17.2 %copy-start.38 = (f32[4,512]{1,0:T(4,128)S(1)}, f32[4,512]{1,0:T(4,128)}, u32[]{:S(2)}) copy-start(f32[4,512]{1,0:T(4,128)} %param.40) | copy-start | bytes 24580
  25.2 17.2 %copy-start.43 = (f32[192]{0:T(256)S(1)}, f32[192]{0:T(256)}, u32[]{:S(2)}) copy-start(f32[192]{0:T(256)} %param.35) | copy-start | bytes 2308
  27.0 15.4 %copy-start.26 = (f32[192]{0:T(256)}, f32[192]{0:T(256)S(1)}, u32[]{:S(2)}) copy-start(f32[192]{0:T(256)S(1)} %get-tuple-element.52) | copy-start | bytes 2308
  27.0 15.4 %copy-start.29 = (f32[192]{0:T(256)}, f32[192]{0:T(256)S(1)}, u32[]{:S(2)}) copy-start(f32[192]{0:T(256)S(1)} %get-tuple-element.53) | copy-start | bytes 2308
  28.6 13.8 %copy-start.24 = (s32[8,16,1]{1,2,0:T(1,128)}, s32[8,16,1]{1,2,0:T(1,128)S(1)}, u32[]{:S(2)}) copy-start(s32[8,16,1]{1,2,0:T(1,128)S(1)} %all-to-all-done) | copy-start | bytes 1540
  28.6 6.7 %all-to-all-start.1 = ((f32[8,16,256]{2,1,0:T(8,128)}), f32[8,16,256]{2,1,0:T(8,128)S(1)}, u32[]{:S(2)}, u32[]{:S(2)}) async-start(f32[8,16,256]{2,1,0:T(8,128)} %bitcast.14), calls=%async_computation.1 | async-start | bytes 262144 | tf_op jit(solution)/shard_map/all_to_all | solution.py:152
  32.1 48.9 %copy-start.21 = (s32[1024]{0:T(1024)}, s32[1024]{0:T(1024)S(1)}, u32[]{:S(2)}) copy-start(s32[1024]{0:T(1024)S(1)} %pad_clamp_fusion.1) | copy-start | bytes 12292
  36.4 14.4 %collective-permute-start.2 = (f32[192,128]{0,1:T(8,128)S(1)}, f32[192,128]{0,1:T(8,128)S(1)}, u32[]{:S(2)}, u32[]{:S(2)}) collective-permute-start(f32[192,128]{0,1:T(8,128)S(1)} %get-tuple-element.21), channel_id=1, source_target_pairs={{0,4},{4,8},{8,12},{12,16},{16,20},{20,24},{24,28},{1,5},{5,9},{9,... | collective-permute-start | bytes 294920 | tf_op jit(solution)/shard_map/ppermute | solution.py:26
  40.4 10.4 %collective-permute-start.3 = (f32[192,128]{0,1:T(8,128)S(1)}, f32[192,128]{0,1:T(8,128)S(1)}, u32[]{:S(2)}, u32[]{:S(2)}) collective-permute-start(f32[192,128]{0,1:T(8,128)S(1)} %get-tuple-element.22), channel_id=1, source_target_pairs={{4,0},{8,4},{12,8},{16,12},{20,16},{24,20},{28,24},{5,1},{9,5},{13... | collective-permute-start | bytes 294920 | tf_op jit(solution)/shard_map/ppermute | solution.py:27
  62.6 7.3 %collective-permute-start.4 = (f32[192,128]{0,1:T(8,128)S(1)}, f32[192,128]{0,1:T(8,128)S(1)}, u32[]{:S(2)}, u32[]{:S(2)}) collective-permute-start(f32[192,128]{0,1:T(8,128)S(1)} %get-tuple-element.19), channel_id=1, source_target_pairs={{0,4},{4,8},{8,12},{12,16},{16,20},{20,24},{24,28},{1,5},{5,9},{9,... | collective-permute-start | bytes 294920 | tf_op jit(solution)/shard_map/ppermute | solution.py:26
  67.1 7.2 %collective-permute-start.5 = (f32[192,128]{0,1:T(8,128)S(1)}, f32[192,128]{0,1:T(8,128)S(1)}, u32[]{:S(2)}, u32[]{:S(2)}) collective-permute-start(f32[192,128]{0,1:T(8,128)S(1)} %get-tuple-element.20), channel_id=1, source_target_pairs={{4,0},{8,4},{12,8},{16,12},{20,16},{24,20},{28,24},{5,1},{9,5},{13... | collective-permute-start | bytes 294920 | tf_op jit(solution)/shard_map/ppermute | solution.py:27
  85.9 5.2 %collective-permute-start.6 = (f32[192,128]{0,1:T(8,128)S(1)}, f32[192,128]{0,1:T(8,128)S(1)}, u32[]{:S(2)}, u32[]{:S(2)}) collective-permute-start(f32[192,128]{0,1:T(8,128)S(1)} %get-tuple-element.17), channel_id=1, source_target_pairs={{0,4},{4,8},{8,12},{12,16},{16,20},{20,24},{24,28},{1,5},{5,9},{9,... | collective-permute-start | bytes 294920 | tf_op jit(solution)/shard_map/ppermute | solution.py:26
  87.8 7.2 %collective-permute-start.7 = (f32[192,128]{0,1:T(8,128)S(1)}, f32[192,128]{0,1:T(8,128)S(1)}, u32[]{:S(2)}, u32[]{:S(2)}) collective-permute-start(f32[192,128]{0,1:T(8,128)S(1)} %get-tuple-element.18), channel_id=1, source_target_pairs={{4,0},{8,4},{12,8},{16,12},{20,16},{24,20},{28,24},{5,1},{9,5},{13... | collective-permute-start | bytes 294920 | tf_op jit(solution)/shard_map/ppermute | solution.py:27
  106.5 5.0 %collective-permute-start.8 = (f32[192,128]{0,1:T(8,128)S(1)}, f32[192,128]{0,1:T(8,128)S(1)}, u32[]{:S(2)}, u32[]{:S(2)}) collective-permute-start(f32[192,128]{0,1:T(8,128)S(1)} %get-tuple-element.15), channel_id=1, source_target_pairs={{0,4},{4,8},{8,12},{12,16},{16,20},{20,24},{24,28},{1,5},{5,9},{9,... | collective-permute-start | bytes 294920 | tf_op jit(solution)/shard_map/ppermute | solution.py:26
  108.5 7.2 %collective-permute-start.9 = (f32[192,128]{0,1:T(8,128)S(1)}, f32[192,128]{0,1:T(8,128)S(1)}, u32[]{:S(2)}, u32[]{:S(2)}) collective-permute-start(f32[192,128]{0,1:T(8,128)S(1)} %get-tuple-element.16), channel_id=1, source_target_pairs={{4,0},{8,4},{12,8},{16,12},{20,16},{24,20},{28,24},{5,1},{9,5},{13... | collective-permute-start | bytes 294920 | tf_op jit(solution)/shard_map/ppermute | solution.py:27
  124.0 13.2 %copy-start.25 = (s32[8,16,1]{1,2,0:T(1,128)S(1)}, s32[8,16,1]{1,2,0:T(1,128)}, u32[]{:S(2)}) copy-start(s32[8,16,1]{1,2,0:T(1,128)} %copy-done.24) | copy-start | bytes 1540
  126.5 20.6 %copy-start.51 = (s32[64]{0:T(128)S(1)}, s32[64]{0:T(128)}, u32[]{:S(2)}) copy-start(s32[64]{0:T(128)} %param.44) | copy-start | bytes 772
  126.5 21.1 %copy-start.12 = (f32[32,512]{1,0:T(8,128)S(1)}, f32[32,512]{1,0:T(8,128)}, u32[]{:S(2)}) copy-start(f32[32,512]{1,0:T(8,128)} %copy-done.11) | copy-start | bytes 196612
  126.5 21.1 %copy-start.17 = (bf16[32,512]{1,0:T(8,128)(2,1)S(1)}, bf16[32,512]{1,0:T(8,128)(2,1)}, u32[]{:S(2)}) copy-start(bf16[32,512]{1,0:T(8,128)(2,1)} %param.26) | copy-start | bytes 98308
  126.5 21.1 %copy-start.18 = (bf16[32,512]{1,0:T(8,128)(2,1)S(1)}, bf16[32,512]{1,0:T(8,128)(2,1)}, u32[]{:S(2)}) copy-start(bf16[32,512]{1,0:T(8,128)(2,1)} %param.25) | copy-start | bytes 98308
  126.5 21.1 %copy-start.1 = (f32[32,512]{1,0:T(8,128)S(1)}, f32[32,512]{1,0:T(8,128)}, u32[]{:S(2)}) copy-start(f32[32,512]{1,0:T(8,128)} %get-tuple-element.36) | copy-start | bytes 196612
  126.5 21.1 %copy-start.2 = (f32[32,512]{1,0:T(8,128)S(1)}, f32[32,512]{1,0:T(8,128)}, u32[]{:S(2)}) copy-start(f32[32,512]{1,0:T(8,128)} %get-tuple-element.37) | copy-start | bytes 196612
  126.5 21.1 %copy-start.9 = (f32[32,512]{1,0:T(8,128)S(1)}, f32[32,512]{1,0:T(8,128)}, u32[]{:S(2)}) copy-start(f32[32,512]{1,0:T(8,128)} %get-tuple-element.60) | copy-start | bytes 196612
  126.5 21.1 %copy-start.10 = (f32[32,512]{1,0:T(8,128)S(1)}, f32[32,512]{1,0:T(8,128)}, u32[]{:S(2)}) copy-start(f32[32,512]{1,0:T(8,128)} %get-tuple-element.61) | copy-start | bytes 196612
  126.5 21.1 %copy-start.14 = (f32[2,32,512]{2,1,0:T(8,128)S(1)}, f32[2,32,512]{2,1,0:T(8,128)}, u32[]{:S(2)}) copy-start(f32[2,32,512]{2,1,0:T(8,128)} %param.24) | copy-start | bytes 393220
  126.5 21.1 %copy-start.15 = (f32[2,32,512]{2,1,0:T(8,128)S(1)}, f32[2,32,512]{2,1,0:T(8,128)}, u32[]{:S(2)}) copy-start(f32[2,32,512]{2,1,0:T(8,128)} %multiply_subtract_fusion.3) | copy-start | bytes 393220
  126.6 21.1 %copy-start.39 = (f32[2]{0:T(128)S(1)}, f32[2]{0:T(128)}, u32[]{:S(2)}) copy-start(f32[2]{0:T(128)} %param.32) | copy-start | bytes 28
  126.6 21.1 %copy-start.40 = (f32[2]{0:T(128)S(1)}, f32[2]{0:T(128)}, u32[]{:S(2)}) copy-start(f32[2]{0:T(128)} %param.33) | copy-start | bytes 28
  126.6 21.1 %copy-start.41 = (f32[2]{0:T(128)S(1)}, f32[2]{0:T(128)}, u32[]{:S(2)}) copy-start(f32[2]{0:T(128)} %param.31) | copy-start | bytes 28
  138.1 7.1 %all-to-all-start.2 = ((f32[8,16,128]{2,1,0:T(8,128)}), f32[8,16,128]{2,1,0:T(8,128)S(1)}, u32[]{:S(2)}, u32[]{:S(2)}) async-start(f32[8,16,128]{2,1,0:T(8,128)} %fusion.104), calls=%async_computation.2 | async-start | bytes 131072 | tf_op jit(solution)/shard_map/all_to_all | solution.py:184
  141.9 13.2 %copy-start.4 = (f32[32,512]{1,0:T(8,128)S(1)}, f32[32,512]{1,0:T(8,128)}, u32[]{:S(2)}) copy-start(f32[32,512]{1,0:T(8,128)} %copy-done.3) | copy-start | bytes 196612
  141.9 13.2 %copy-start.6 = (f32[32,512]{1,0:T(8,128)S(1)}, f32[32,512]{1,0:T(8,128)}, u32[]{:S(2)}) copy-start(f32[32,512]{1,0:T(8,128)} %copy-done.5) | copy-start | bytes 196612
  141.9 13.2 %copy-start.8 = (f32[32,512]{1,0:T(8,128)S(1)}, f32[32,512]{1,0:T(8,128)}, u32[]{:S(2)}) copy-start(f32[32,512]{1,0:T(8,128)} %copy-done.7) | copy-start | bytes 196612
  148.6 6.6 %collective-permute-start.10 = (f32[2,1,512]{2,1,0:T(1,128)S(1)}, f32[2,1,512]{2,1,0:T(1,128)S(1)}, u32[]{:S(2)}, u32[]{:S(2)}) collective-permute-start(f32[2,1,512]{2,1,0:T(1,128)S(1)} %get-tuple-element.27), channel_id=1, source_target_pairs={{4,0},{8,4},{12,8},{16,12},{20,16},{24,20},{28,24},{5,1},{9,5},{13... | collective-permute-start | bytes 12296 | tf_op jit(solution)/shard_map/ppermute | solution.py:27
  151.1 4.7 %collective-permute-start.11 = (f32[2,1,512]{2,1,0:T(1,128)S(1)}, f32[2,1,512]{2,1,0:T(1,128)S(1)}, u32[]{:S(2)}, u32[]{:S(2)}) collective-permute-start(f32[2,1,512]{2,1,0:T(1,128)S(1)} %get-tuple-element.28), channel_id=1, source_target_pairs={{0,4},{4,8},{8,12},{12,16},{16,20},{20,24},{24,28},{1,5},{5,9},{9,... | collective-permute-start | bytes 12296 | tf_op jit(solution)/shard_map/ppermute | solution.py:26
  155.9 7.1 %collective-permute-start.12 = (f32[2,1,512]{2,1,0:T(1,128)S(1)}, f32[2,1,512]{2,1,0:T(1,128)S(1)}, u32[]{:S(2)}, u32[]{:S(2)}) collective-permute-start(f32[2,1,512]{2,1,0:T(1,128)S(1)} %get-tuple-element.25), channel_id=1, source_target_pairs={{4,0},{8,4},{12,8},{16,12},{20,16},{24,20},{28,24},{5,1},{9,5},{13... | collective-permute-start | bytes 12296 | tf_op jit(solution)/shard_map/ppermute | solution.py:27
  158.8 4.9 %collective-permute-start.13 = (f32[2,1,512]{2,1,0:T(1,128)S(1)}, f32[2,1,512]{2,1,0:T(1,128)S(1)}, u32[]{:S(2)}, u32[]{:S(2)}) collective-permute-start(f32[2,1,512]{2,1,0:T(1,128)S(1)} %get-tuple-element.26), channel_id=1, source_target_pairs={{0,4},{4,8},{8,12},{12,16},{16,20},{20,24},{24,28},{1,5},{5,9},{9,... | collective-permute-start | bytes 12296 | tf_op jit(solution)/shard_map/ppermute | solution.py:26
  163.9 7.1 %collective-permute-start.14 = (f32[2,1,512]{2,1,0:T(1,128)S(1)}, f32[2,1,512]{2,1,0:T(1,128)S(1)}, u32[]{:S(2)}, u32[]{:S(2)}) collective-permute-start(f32[2,1,512]{2,1,0:T(1,128)S(1)} %get-tuple-element.23), channel_id=1, source_target_pairs={{4,0},{8,4},{12,8},{16,12},{20,16},{24,20},{28,24},{5,1},{9,5},{13... | collective-permute-start | bytes 12296 | tf_op jit(solution)/shard_map/ppermute | solution.py:27
  165.8 5.8 %collective-permute-start.15 = (f32[2,1,512]{2,1,0:T(1,128)S(1)}, f32[2,1,512]{2,1,0:T(1,128)S(1)}, u32[]{:S(2)}, u32[]{:S(2)}) collective-permute-start(f32[2,1,512]{2,1,0:T(1,128)S(1)} %get-tuple-element.24), channel_id=1, source_target_pairs={{0,4},{4,8},{8,12},{12,16},{16,20},{20,24},{24,28},{1,5},{5,9},{9,... | collective-permute-start | bytes 12296 | tf_op jit(solution)/shard_map/ppermute | solution.py:26
  (24 other events, 107.8 us)
where the time goes:
time: 175 us; the launch traced here: 172 us
  starting transfers between devices  59.8 us (34%)
  local copies, waits for them, and re-layouts  44.7 us (26%)
  other arithmetic  33.7 us (19%)
  waiting for transfers between devices  18 us (10%)
  blocking collectives  9.92 us (6%)
  matrix products  4.54 us (3%)
  between operations  1.75 us (1%)
    gather x16, local copies, waits for them, and re-layouts, per_device(): jnp.take(padded, local_index[neighbor], axis=1)  35 us
    ppermute x8, starting transfers between devices, with_halo(): before = lax.ppermute(last, axis, up)  29.8 us
    ppermute x8, starting transfers between devices, with_halo(): after = lax.ppermute(first, axis, down)  18.3 us
    ppermute x8, waiting for transfers between devices, with_halo(): after = lax.ppermute(first, axis, down)  12.5 us
    psum x1, blocking collectives, per_device(): orbital = lax.psum(jnp.dot(coefficient, energy, precision=HIGHEST), 'lev')  9.92 us
    mul x1, other arithmetic, band_rates(): base_rate[None]  8.46 us
    mul x3, other arithmetic, per_device(): energy = (energy + arriving - total_rate * energy) * alive_mask  7.72 us
    all_to_all x1, starting transfers between devices, per_device(): lax.all_to_all(send_ids, ('sec', 'tile'), split_axis=0, concat_axis=0, ti...  4.57 us
  transfers between devices with their start and end apart: 19, of which 8 were waited for; matrix products, arithmetic and copies ran while one was open for 44% of the time, Pallas kernels for 0%

commit v1 on v0

v1 whole, which is shorter than its diff:
```python
import functools

import jax
import jax.numpy as jnp
from jax import lax
from jax.experimental import pallas as pl
from jax.experimental.pallas import tpu as pltpu
from jax.sharding import PartitionSpec as P

OSTEPS = 4
WSTEPS = 4
NBRS = 4
KAPPA = 0.07
FORCE_SCALE = 5.0
DRAG = 50.0
TAU_CURRENT = 20.0
TAU_WAVES = 10.0
MESH = pl.DeviceIdType.MESH
F32 = jnp.float32
BF16 = jnp.bfloat16


def parts(x):
    hi = x.astype(BF16)
    lo = (x - hi.astype(F32)).astype(BF16)
    return hi, lo


def two(x, axis):
    return jnp.concatenate(parts(x), axis=axis)


def dot(a, b):
    return jnp.dot(a, b, preferred_element_type=F32)


def fold(x):
    total = x[:, 0:128]
    for i in range(1, x.shape[1] // 128):
        total = total + x[:, 128 * i : 128 * i + 128]
    return total + pltpu.roll(total, 64, axis=1)


def iota(shape, dim):
    return lax.broadcasted_iota(jnp.int32, shape, dim)


def kernel(
    sizes,
    conc, flow_lo, flow_hi, flow_y, open_lo, open_hi, open_y,
    settle, critical, erosion,
    wave, bands, meta_in, ent_cols, ent_rows, weight,
    sed_out, wave_out,
    we, meta, conc_x, fields, tau_x, table, table_in, wf,
    select, inflow, keep, energy, split, orb, orb_in, gathered,
    halo_send, halo_recv, table_send, table_recv, lev_send, lev_recv, orb_send, orb_recv,
):
    n_tile, n, n_lev = sizes
    bins = wave.shape[0]
    rows, cols = flow_lo.shape
    ent = ent_cols.shape[0]
    pairs = 4 * n
    classes = conc.shape[0]
    sec, tile, lev = lax.axis_index("sec"), lax.axis_index("tile"), lax.axis_index("lev")
    me = sec * n_tile + tile

    def plane(peer):
        return {"sec": peer // n_tile, "tile": lax.rem(peer, n_tile)}

    barrier = pltpu.get_barrier_semaphore()

    @pl.loop(1, n)
    def _(off):
        pl.semaphore_signal(
            barrier, inc=1, device_id=plane(lax.rem(me + off, n)), device_id_type=MESH
        )

    @pl.loop(1, n_lev)
    def _(off):
        pl.semaphore_signal(
            barrier, inc=1, device_id={"lev": lax.rem(lev + off, n_lev)}, device_id_type=MESH
        )

    for j in range(4):
        we[4 + j] = wave[:, 128 * j : 128 * j + 128].astype(F32)
        meta[4 + j] = meta_in[:, 128 * j : 128 * j + 128]

    lo, hi, side = flow_lo[...].astype(F32), flow_hi[...].astype(F32), flow_y[...].astype(F32)
    ol, oh, oy = open_lo[...].astype(F32), open_hi[...].astype(F32), open_y[...].astype(F32)
    first_col = iota((rows, cols), 1) == 0

    def left_of(x):
        return jnp.where(first_col, 0.0, pltpu.roll(x, 1, axis=1))

    east = 0.5 * (lo + hi)
    north = 0.5 * (side + left_of(side))
    square = east * east + north * north
    speed = jnp.sqrt(square)
    a_y = jnp.maximum(side, 0.0) + KAPPA * oy
    b_y = jnp.minimum(side, 0.0) - KAPPA * oy
    a_hi = jnp.maximum(hi, 0.0) + KAPPA * oh
    b_hi = jnp.minimum(hi, 0.0) - KAPPA * oh
    a_lo = jnp.maximum(lo, 0.0) + KAPPA * ol
    b_lo = jnp.minimum(lo, 0.0) - KAPPA * ol
    mid = pl.ds(8, rows)
    fields[0, mid] = 1.0 - a_hi + b_lo - a_y + left_of(b_y)
    fields[1, mid] = a_lo
    fields[2, mid] = -b_hi
    fields[3, mid] = -b_y
    fields[4, mid] = left_of(a_y)
    fields[5, mid] = TAU_CURRENT * square
    for c in range(classes):
        conc_x[c, mid] = conc[c]

    @pl.when(me == 0)
    def _():
        we[0:4] = jnp.zeros((4, bins, 128), F32)
        meta[0:4] = jnp.zeros((4, 16, 128), F32)
        fields[:, 0:8] = jnp.zeros((6, 8, cols), F32)
        conc_x[:, 0:8] = jnp.zeros((classes, 8, cols), F32)
        tau_x[0:8] = jnp.zeros((8, cols), F32)

    @pl.when(me == n - 1)
    def _():
        we[8:12] = jnp.zeros((4, bins, 128), F32)
        meta[8:12] = jnp.zeros((4, 16, 128), F32)
        fields[:, rows + 8 : rows + 16] = jnp.zeros((6, 8, cols), F32)
        conc_x[:, rows + 8 : rows + 16] = jnp.zeros((classes, 8, cols), F32)
        tau_x[rows + 8 : rows + 16] = jnp.zeros((8, cols), F32)

    pl.semaphore_wait(barrier, n - 1 + n_lev - 1)

    def to_right(src, dst, i):
        return pltpu.make_async_remote_copy(
            src_ref=src, dst_ref=dst,
            send_sem=halo_send.at[0, i], recv_sem=halo_recv.at[0, i],
            device_id=plane(lax.rem(me + 1, n)), device_id_type=MESH,
        )

    def to_left(src, dst, i):
        return pltpu.make_async_remote_copy(
            src_ref=src, dst_ref=dst,
            send_sem=halo_send.at[1, i], recv_sem=halo_recv.at[1, i],
            device_id=plane(lax.rem(me + n - 1, n)), device_id_type=MESH,
        )

    own, before, after = pl.ds(4, 4), pl.ds(0, 4), pl.ds(8, 4)
    top, bottom = pl.ds(8, 8), pl.ds(rows, 8)
    above, below = pl.ds(0, 8), pl.ds(rows + 8, 8)
    right = [
        to_right(meta.at[own], meta.at[before], 0),
        to_right(we.at[own], we.at[before], 1),
        to_right(fields.at[:, bottom], fields.at[:, above], 2),
        to_right(conc_x.at[:, bottom], conc_x.at[:, above], 3),
        to_right(tau_x.at[bottom], tau_x.at[above], 4),
    ]
    left = [
        to_left(meta.at[own], meta.at[after], 0),
        to_left(we.at[own], we.at[after], 1),
        to_left(fields.at[:, top], fields.at[:, below], 2),
        to_left(conc_x.at[:, top], conc_x.at[:, below], 3),
        to_left(tau_x.at[top], tau_x.at[below], 4),
    ]

    def start(items):
        @pl.when(me < n - 1)
        def _():
            for i in items:
                right[i].start()

        @pl.when(me > 0)
        def _():
            for i in items:
                left[i].start()

    def arrived(items):
        @pl.when(me > 0)
        def _():
            for i in items:
                right[i].wait_recv()

        @pl.when(me < n - 1)
        def _():
            for i in items:
                left[i].wait_recv()

    def sent(items):
        @pl.when(me < n - 1)
        def _():
            for i in items:
                right[i].wait_send()

        @pl.when(me > 0)
        def _():
            for i in items:
                left[i].wait_send()

    start([0, 1])

    cell_row, cell_col = ent_cols[:, 0:1], ent_cols[:, 1:2]
    pair_col, parity = ent_cols[:, 2:3], ent_cols[:, 3:4]
    row_hot = (iota((ent, rows), 1) == cell_row).astype(F32).astype(BF16)
    forcing = jnp.concatenate(
        [
            FORCE_SCALE * east,
            FORCE_SCALE * north,
            DRAG * speed * east,
            DRAG * speed * north,
        ],
        axis=1,
    )
    picked = dot(jnp.concatenate([row_hot, row_hot], axis=1), two(forcing, 0))
    cell_mask = (iota((ent, cols), 1) // 64 == cell_col).astype(F32)
    channels = [fold(picked[:, cols * c : cols * c + cols] * cell_mask)[:, 0:64] for c in range(4)]
    group_mask = (iota((32, 512), 1) // 64 == lax.rem(iota((32, 512), 0), 8)).astype(F32)
    pieces = []
    for g in range(ent // 8):
        left_side = two(jnp.concatenate([x[8 * g : 8 * g + 8] for x in channels], axis=0), 0)
        block = lax.dot_general(
            left_side, weight[512 * g : 512 * g + 512, :],
            (((1,), (1,)), ((), ())), preferred_element_type=F32,
        )
        pieces.append(fold((block[0:32] + block[32:64]) * group_mask))
    parity_mask = (iota((ent, 128), 1) // 64 == parity).astype(F32)
    stacked = jnp.concatenate(
        [
            jnp.concatenate([x[8 * c : 8 * c + 8] for x in pieces], axis=0) * parity_mask
            for c in range(4)
        ],
        axis=1,
    )
    pair_hot = (iota((pairs, ent), 0) == ent_rows[0:1, :]).astype(F32).astype(BF16)
    sums = dot(jnp.concatenate([pair_hot, pair_hot], axis=1), two(stacked, 0))
    table[0:4] = jnp.zeros((4, 4, 128), F32)
    table[pairs + 4 : pairs + 8] = jnp.zeros((4, 4, 128), F32)
    for c in range(4):
        table[4 : pairs + 4, c, :] = sums[:, 128 * c : 128 * c + 128]

    def table_copy(off):
        peer = lax.rem(me + off, n)
        return pltpu.make_async_remote_copy(
            src_ref=table.at[pl.ds(4 * peer, 12)], dst_ref=table_in.at[off],
            send_sem=table_send.at[off], recv_sem=table_recv.at[off],
            device_id=plane(peer), device_id_type=MESH,
        )

    @pl.loop(1, n)
    def _(off):
        table_copy(off).start()

    start([2, 3])

    arrived([0])

    @pl.loop(1, 11)
    def _(b):
        base = (4 * me - 5 + b) * 128
        near = meta[b][0:NBRS].astype(jnp.int32) - base
        for k in range(NBRS):
            hot = (iota((384, 128), 0) == near[k : k + 1, :]).astype(F32)
            select[b, :, 128 * k : 128 * k + 128] = hot.astype(BF16)

    arrived([1])
    wf[...] = table[pl.ds(4 * me, 12)]

    @pl.loop(1, n)
    def _(off):
        table_copy(off).wait_recv()
        wf[...] += table_in[off]

    cosine, sine = bands[:, 0:1], bands[:, 1:2]
    pace, growth = bands[:, 2:3], bands[:, 3:4]
    coef_c, coef_s = bands[:, 4:5], bands[:, 5:6]

    @pl.loop(0, 12)
    def _(b):
        w = wf[b]
        m = meta[b]
        alive = m[12:13, :]
        push = jnp.maximum(cosine * w[2:3, :] + sine * w[3:4, :], 0.0)
        first = (we[b] + growth * push) * alive
        energy[b] = first
        split[0, b] = two(first, 0)
        drift = cosine * w[0:1, :] + sine * w[1:2, :]
        rate = pace * (0.5 + 0.25 * jnp.tanh(drift)) * alive
        total = jnp.zeros((bins, 128), F32)
        for k in range(NBRS):
            flow = rate * jnp.maximum(
                -(cosine * m[4 + k : 5 + k, :] + sine * m[8 + k : 9 + k, :]), 0.0
            )
            inflow[b, k] = flow
            total = total + flow
        keep[b] = alive - total

    for step in range(WSTEPS):
        now, later = step % 2, (step + 1) % 2

        @pl.loop(step + 1, 11 - step)
        def _(b):
            window = jnp.concatenate(
                [split[now, b - 1], split[now, b], split[now, b + 1]], axis=1
            )
            got = dot(window, select[b])
            new = keep[b] * energy[b]
            for k in range(NBRS):
                lanes = slice(128 * k, 128 * k + 128)
                new = new + inflow[b, k] * (got[0:bins, lanes] + got[bins : 2 * bins, lanes])
            energy[b] = new
            if step < WSTEPS - 1:
                split[later, b] = two(new, 0)

    for j in range(4):
        final = energy[4 + j]
        orb[j, 0:1, :] = jnp.sum(coef_c * final, axis=0, keepdims=True)
        orb[j, 1:2, :] = jnp.sum(coef_s * final, axis=0, keepdims=True)

    def lev_copy(off):
        return pltpu.make_async_remote_copy(
            src_ref=orb, dst_ref=orb_in.at[off],
            send_sem=lev_send.at[off], recv_sem=lev_recv.at[off],
            device_id={"lev": lax.rem(lev + off, n_lev)}, device_id_type=MESH,
        )

    for off in range(1, n_lev):
        lev_copy(off).start()
    for j in range(4):
        wave_out[:, 128 * j : 128 * j + 128] = energy[4 + j].astype(BF16)
    full = orb[...]
    for off in range(1, n_lev):
        lev_copy(off).wait_recv()
        full = full + orb_in[off]
    mine = pl.ds(4 * me, 4)
    gathered[mine] = full

    def orb_copy(off):
        return pltpu.make_async_remote_copy(
            src_ref=gathered.at[mine], dst_ref=gathered.at[mine],
            send_sem=orb_send.at[off], recv_sem=orb_recv.at[off],
            device_id=plane(lax.rem(me + off, n)), device_id_type=MESH,
        )

    def orb_arrival(off):
        source = pl.ds(4 * lax.rem(me - off + n, n), 4)
        return pltpu.make_async_remote_copy(
            src_ref=gathered.at[mine], dst_ref=gathered.at[source],
            send_sem=orb_send.at[off], recv_sem=orb_recv.at[off],
            device_id=plane(lax.rem(me + off, n)), device_id_type=MESH,
        )

    @pl.loop(1, n)
    def _(off):
        orb_copy(off).start()

    hot = (iota((ent, pairs), 1) == pair_col).astype(F32).astype(BF16)
    group_mask = (iota((ent, 512), 1) // 64 == lax.rem(iota((ent, 512), 0), 8)).astype(F32)

    @pl.loop(1, n)
    def _(off):
        orb_arrival(off).wait_recv()

    field = jnp.concatenate([gathered[:, 0, :], gathered[:, 1, :]], axis=1)
    back = dot(jnp.concatenate([hot, hot], axis=1), two(field, 0))
    wide = []
    for c in range(2):
        x = fold(back[:, 128 * c : 128 * c + 128] * parity_mask)
        wide.append(jnp.concatenate([x, x, x, x], axis=1) * group_mask)
    spread = []
    for g in range(ent // 8):
        left_side = two(jnp.concatenate([x[8 * g : 8 * g + 8] for x in wide], axis=0), 0)
        block = dot(left_side, weight[512 * g : 512 * g + 512, :])
        spread.append(block[0:16] + block[16:32])
    row_hot_t = (iota((rows, ent), 0) == ent_rows[1:2, :]).astype(F32).astype(BF16)
    placed = []
    for c in range(2):
        x = jnp.concatenate([y[8 * c : 8 * c + 8] for y in spread], axis=0)
        placed.append(jnp.concatenate([x] * (cols // 64), axis=1) * cell_mask)
    orbital = dot(
        jnp.concatenate([row_hot_t, row_hot_t], axis=1), two(jnp.concatenate(placed, axis=1), 0)
    )
    orbital_c, orbital_s = orbital[:, 0:cols], orbital[:, cols : 2 * cols]
    tau_x[mid] = TAU_WAVES * (orbital_c * orbital_c + orbital_s * orbital_s)
    start([4])
    arrived([2, 3, 4])
    stress = fields[5] + tau_x[...]
    tall = rows + 16
    for c in range(classes):
        gain = erosion[c] * jnp.maximum(stress / critical[c] - 1.0, 0.0)
        centre = fields[0] - settle[c]
        state = conc_x[c]
        for _ in range(OSTEPS):
            state = (
                centre * state
                + fields[1] * pltpu.roll(state, 1, axis=0)
                + fields[2] * pltpu.roll(state, tall - 1, axis=0)
                + fields[3] * pltpu.roll(state, cols - 1, axis=1)
                + fields[4] * pltpu.roll(state, 1, axis=1)
                + gain
            )
        sed_out[c] = state[8 : rows + 8]

    sent([0, 1, 2, 3, 4])

    @pl.loop(1, n)
    def _(off):
        table_copy(off).wait_send()
        orb_copy(off).wait_send()

    for off in range(1, n_lev):
        lev_copy(off).wait_send()


def per_device(
    ocean_conc, flow_lo, flow_hi, flow_y, open_lo, open_hi, open_y,
    settle_rate, critical_stress, erosion_rate,
    wave_energy, band_angle, band_speed, band_growth, band_orbital,
    neighbors, facing_angle, live_nodes,
    remap_owner, remap_slot, remap_cell, remap_weight,
):
    n_tile = lax.axis_size("tile")
    n = lax.axis_size("sec") * n_tile
    n_lev = lax.axis_size("lev")
    rows, cols = flow_lo.shape
    bins, nodes = wave_energy.shape
    ent = remap_cell.shape[0]
    classes = ocean_conc.shape[0]
    pairs = 4 * n
    per_row = cols // 64
    cosine, sine = jnp.cos(band_angle), jnp.sin(band_angle)
    nothing = jnp.zeros_like(cosine)
    bands = jnp.stack(
        [cosine, sine, band_speed, band_growth, band_orbital * cosine, band_orbital * sine,
         nothing, nothing],
        axis=1,
    )
    meta = jnp.concatenate(
        [
            neighbors.astype(F32),
            jnp.cos(facing_angle),
            jnp.sin(facing_angle),
            live_nodes.astype(F32)[None],
            jnp.zeros((3, nodes), F32),
        ],
        axis=0,
    )
    owner = remap_owner[:, 0]
    pair = owner * 4 + remap_slot // 2
    ent_cols = jnp.stack(
        [remap_cell // per_row, remap_cell % per_row, pair, remap_slot % 2], axis=1
    )
    ent_rows = jnp.stack([pair, remap_cell // per_row], axis=0)
    vmem = pl.BlockSpec(memory_space=pltpu.VMEM)
    smem = pl.BlockSpec(memory_space=pltpu.SMEM)
    tall = rows + 16
    return pl.pallas_call(
        functools.partial(kernel, (n_tile, n, n_lev)),
        out_shape=(
            jax.ShapeDtypeStruct(ocean_conc.shape, F32),
            jax.ShapeDtypeStruct(wave_energy.shape, BF16),
        ),
        in_specs=[vmem] * 7 + [smem] * 3 + [vmem] * 6,
        out_specs=(vmem, vmem),
        scratch_shapes=[
            pltpu.VMEM((12, bins, 128), F32),
            pltpu.VMEM((12, 16, 128), F32),
            pltpu.VMEM((classes, tall, cols), F32),
            pltpu.VMEM((6, tall, cols), F32),
            pltpu.VMEM((tall, cols), F32),
            pltpu.VMEM((pairs + 8, 4, 128), F32),
            pltpu.VMEM((n, 12, 4, 128), F32),
            pltpu.VMEM((12, 4, 128), F32),
            pltpu.VMEM((12, 384, 512), BF16),
            pltpu.VMEM((12, NBRS, bins, 128), F32),
            pltpu.VMEM((12, bins, 128), F32),
            pltpu.VMEM((12, bins, 128), F32),
            pltpu.VMEM((2, 12, 2 * bins, 128), BF16),
            pltpu.VMEM((4, 2, 128), F32),
            pltpu.VMEM((n_lev, 4, 2, 128), F32),
            pltpu.VMEM((pairs, 2, 128), F32),
            pltpu.SemaphoreType.DMA((2, 5)),
            pltpu.SemaphoreType.DMA((2, 5)),
            pltpu.SemaphoreType.DMA((n,)),
            pltpu.SemaphoreType.DMA((n,)),
            pltpu.SemaphoreType.DMA((n_lev,)),
            pltpu.SemaphoreType.DMA((n_lev,)),
            pltpu.SemaphoreType.DMA((n,)),
            pltpu.SemaphoreType.DMA((n,)),
        ],
        compiler_params=pltpu.CompilerParams(
            collective_id=0, has_side_effects=True, vmem_limit_bytes=48 * 1024 * 1024
        ),
    )(
        ocean_conc, flow_lo, flow_hi, flow_y, open_lo, open_hi, open_y,
        settle_rate, critical_stress, erosion_rate,
        wave_energy, bands, meta, ent_cols, ent_rows, remap_weight.reshape(ent * 64, 64),
    )


def solution(mesh):
    both = ("sec", "tile")
    return jax.shard_map(
        per_device,
        mesh=mesh,
        in_specs=(
            P("lev", both, None),
            P(both, None),
            P(both, None),
            P(both, None),
            P(both, None),
            P(both, None),
            P(both, None),
            P("lev"),
            P("lev"),
            P("lev"),
            P("lev", both),
            P("lev"),
            P("lev"),
            P("lev"),
            P("lev"),
            P(None, both),
            P(None, both),
            P(both),
            P(both, None),
            P(both),
            P(both),
            P(both, None, None),
        ),
        out_specs=(P("lev", both, None), P("lev", both)),
        check_vma=False,
    )
```

time: 175 us -> 57.6 us (0.33); the launches traced: 172 us -> 56.9 us
  starting transfers between devices: 59.8 us -> 0 us
  Pallas kernels: 0 us -> 43 us
  local copies, waits for them, and re-layouts: 44.7 us -> 10.4 us
  other arithmetic: 33.7 us -> 2.87 us
  waiting for transfers between devices: 18 us -> 0 us
  blocking collectives: 9.92 us -> 0 us
  matrix products: 4.54 us -> 0 us
    ppermute x16 -> x0, starting transfers between devices: 48.1 us -> none  [the longest x8 29.8 us: with_halo(): before = lax.ppermute(last, axis, up)]
    pallas_call x0 -> x1, Pallas kernels: none -> 43 us  [per_device(): pl.pallas_call(functools.partial(kernel, (n_tile, n, n_lev)), out_shape=(...]
    gather x18 -> x0, local copies, waits for them, and re-layouts: 36.2 us -> none  [the longest x16 35 us: per_device(): jnp.take(padded, local_index[neighbor], axis=1)]
    mul x10 -> x1, other arithmetic: 19.5 us -> 0.69 us  [per_device(): band_orbital * sine]
    ppermute x16 -> x0, waiting for transfers between devices: 14.3 us -> none  [the longest x8 12.5 us: with_halo(): after = lax.ppermute(first, axis, down)]
    all_to_all x3 -> x0, starting transfers between devices: 11.7 us -> none  [the longest x1 4.57 us: per_device(): lax.all_to_all(send_ids, ('sec', 'tile'), split_axis=0, concat_axis=0, ti...]
    psum x1 -> x0, blocking collectives: 9.92 us -> none  [per_device(): orbital = lax.psum(jnp.dot(coefficient, energy, precision=HIGHEST), 'lev')]
    unnamed x108 -> x26, local copies, waits for them, and re-layouts: 1.79 us -> 7.89 us
  transfers between devices with their start and end apart: 19 -> 0, of which waited for: 8 -> 0; matrix products, arithmetic and copies ran while one was open for 44% -> 0% of each run, Pallas kernels for 0% -> 0%
where the time goes in v1:
time: 57.6 us; the launch traced here: 56.9 us
  Pallas kernels  43 us (75%)
  local copies, waits for them, and re-layouts  10.4 us (18%)
  other arithmetic  2.87 us (5%)
  between operations  0.73 us (1%)
    pallas_call x1, Pallas kernels, per_device(): pl.pallas_call(functools.partial(kernel, (n_tile, n, n_lev)), out_shape=(...  43 us
    unnamed x26, local copies, waits for them, and re-layouts  7.89 us

profile of v1, /device:TPU:3, one launch (start us, length us, event | category | flops | bytes accessed | tf_op | source)
XLA Modules:
  0.0 56.9 jit_solution(529600554900992711)
XLA Ops:
  0.6 0.0 copy-start.1
  0.6 0.7 %convert_element_type.7 = f32[512]{0:T(512)S(1)} convert(s32[512]{0:T(512)} %param.39) | non-fusion elementwise | flops 512 | bytes 4096 | tf_op jit(solution)/shard_map/convert_element_type | solution.py:440
  1.4 0.7 %and_select_fusion.3 = (s32[64]{0:T(128)S(1)}, s32[64,1]{0,1:T(1,128)S(1)}, s32[64,1]{0,1:T(1,128)S(1)}, s32[64]{0:T(128)S(1)}) fusion(s32[64]{0:T(128)} %param.42, s32[64]{0:T(128)} %param.41, s32[64,1]{0,1:T(1,128)} %param.40), kind=kLoop, calls=%fused_computation.4 | loop fusion | flops 2560 | bytes 1792 | tf_op jit(solution)/shard_map/jit(floor_divide)/jit(_where)/select_n | solution.py:448
  2.1 0.7 %fusion.4 = (f32[192]{0:T(256)S(1)}, f32[192]{0:T(256)S(1)}) fusion(f32[192]{0:T(256)} %param.33), kind=kLoop, calls=%fused_computation.17 | loop fusion | bytes 2304 | tf_op jit(solution)/shard_map/sin | solution.py:428
  2.8 0.7 %fusion.3 = (f32[192]{0:T(256)S(1)}, f32[192]{0:T(256)S(1)}) fusion(f32[192]{0:T(256)} %param.36, f32[192]{0:T(256)S(1)} %get-tuple-element.6, f32[192]{0:T(256)S(1)} %get-tuple-element.7), kind=kLoop, calls=%fused_computation.16 | loop fusion | flops 384 | bytes 3840 | tf_op jit(solution)/shard_map/mul | solution.py:431
  3.5 0.7 %stack.55 = f32[192,8]{0,1:T(8,128)S(1)} concatenate(f32[192,1]{0,1:T(1,128)S(1)} %bitcast.20, f32[192,1]{0,1:T(1,128)S(1)} %bitcast.19, f32[192,1]{0,1:T(1,128)} %bitcast.28, f32[192,1]{0,1:T(1,128)} %bitcast.29, f32[192,1]{0,1:T(1,128)S(1)} %bitcast.27, f32[192,1]{0,1:T(1,128)S(1)} %bitcast.26, f32[192,2]{0,1:T(2,128)S(1)} %stack.54), dimensions={1} | concatenate | bytes 12288 | tf_op jit(solution)/shard_map/stack | solution.py:430
  4.2 0.0 copy-start.2
  4.2 0.7 %convert_element_type.6 = f32[4,512]{1,0:T(4,128)S(1)} convert(s32[4,512]{1,0:T(4,128)} %param.37) | non-fusion elementwise | flops 2048 | bytes 16384 | tf_op jit(solution)/shard_map/convert_element_type | solution.py:437
  5.0 0.8 %fusion.2 = (f32[4,512]{1,0:T(4,128)S(1)}, f32[4,512]{1,0:T(4,128)S(1)}) fusion(f32[4,512]{1,0:T(4,128)} %param.38), kind=kLoop, calls=%fused_computation.15 | loop fusion | bytes 24576 | tf_op jit(solution)/shard_map/sin | solution.py:439
  5.8 0.1 copy.39.ent_cols
  5.9 0.0 copy-start.9
  5.9 0.0 copy-start.10
  5.9 0.0 copy-start.11
  5.9 0.1 copy.38.bands
  6.0 0.0 copy-done.1
  6.0 0.0 copy-done.2
  6.1 0.5 copy-done.9
  6.6 0.0 copy-done.10
  6.6 0.0 copy-done.11
  6.6 0.0 copy-start
  6.6 1.2 %copy-done = bf16[64,64,64]{2,1,0:T(8,128)(2,1)S(1)} copy-done((bf16[64,64,64]{2,1,0:T(8,128)(2,1)S(1)}, bf16[64,64,64]{2,1,0:T(8,128)(2,1)}, u32[]{:S(2)}) %copy-start) | copy-done | bytes 524312
  7.8 0.0 copy-start.3
  7.8 0.8 %copy-done.3 = s32[32,512]{1,0:T(8,128)S(1)} copy-done((s32[32,512]{1,0:T(8,128)S(1)}, s32[32,512]{1,0:T(8,128)}, u32[]{:S(2)}) %copy-start.3) | copy-done | bytes 65560
  8.7 0.0 copy-start.4
  8.7 0.8 %copy-done.4 = s32[32,512]{1,0:T(8,128)S(1)} copy-done((s32[32,512]{1,0:T(8,128)S(1)}, s32[32,512]{1,0:T(8,128)}, u32[]{:S(2)}) %copy-start.4) | copy-done | bytes 65560
  9.5 0.0 copy-start.5
  9.5 0.8 %copy-done.5 = s32[32,512]{1,0:T(8,128)S(1)} copy-done((s32[32,512]{1,0:T(8,128)S(1)}, s32[32,512]{1,0:T(8,128)}, u32[]{:S(2)}) %copy-start.5) | copy-done | bytes 65560
  10.3 0.0 copy-start.6
  10.3 0.8 %copy-done.6 = bf16[32,512]{1,0:T(8,128)(2,1)S(1)} copy-done((bf16[32,512]{1,0:T(8,128)(2,1)S(1)}, bf16[32,512]{1,0:T(8,128)(2,1)}, u32[]{:S(2)}) %copy-start.6) | copy-done | bytes 32792
  11.1 0.0 copy-start.7
  11.1 0.8 %copy-done.7 = bf16[32,512]{1,0:T(8,128)(2,1)S(1)} copy-done((bf16[32,512]{1,0:T(8,128)(2,1)S(1)}, bf16[32,512]{1,0:T(8,128)(2,1)}, u32[]{:S(2)}) %copy-start.7) | copy-done | bytes 32792
  11.8 0.0 copy-start.8
  11.8 0.8 %copy-done.8 = bf16[32,512]{1,0:T(8,128)(2,1)S(1)} copy-done((bf16[32,512]{1,0:T(8,128)(2,1)S(1)}, bf16[32,512]{1,0:T(8,128)(2,1)}, u32[]{:S(2)}) %copy-start.8) | copy-done | bytes 32792
  12.6 43.0 %shard_map.221 = (f32[2,32,512]{2,1,0:T(8,128)S(1)}, bf16[192,512]{1,0:T(8,128)(2,1)S(1)}) custom-call(f32[2,32,512]{2,1,0:T(8,128)S(1)} %copy-done.2, bf16[32,512]{1,0:T(8,128)(2,1)S(1)} %copy-done.6, bf16[32,512]{1,0:T(8,128)(2,1)S(1)} %copy-done.7, bf16[32,512]{1,0:T(8,128)(2,1)S(1)} %copy-done.8, s32[32,512]{1,0:T(8,128)S(1)} %copy-done.3, ...), custom_call_target="tpu_custom_call" | custom-call | tf_op jit(solution)/shard_map/pallas_call | solution.py:454
  55.6 0.7 %copy.42 = f32[2,32,512]{2,1,0:T(8,128)} copy(f32[2,32,512]{2,1,0:T(8,128)S(1)} %get-tuple-element.16) | data formatting | bytes 262144
  56.3 0.7 %copy.43 = bf16[192,512]{1,0:T(8,128)(2,1)} copy(bf16[192,512]{1,0:T(8,128)(2,1)S(1)} %get-tuple-element.17) | data formatting | bytes 393216
  (5 shorter events, 0.1 us)
Async XLA Ops:
  0.6 5.4 %copy-start.1 = (bf16[192,512]{1,0:T(8,128)(2,1)S(1)}, bf16[192,512]{1,0:T(8,128)(2,1)}, u32[]{:S(2)}) copy-start(bf16[192,512]{1,0:T(8,128)(2,1)} %wave.1) | copy-start | bytes 589828
  4.2 1.8 %copy-start.2 = (f32[2,32,512]{2,1,0:T(8,128)S(1)}, f32[2,32,512]{2,1,0:T(8,128)}, u32[]{:S(2)}) copy-start(f32[2,32,512]{2,1,0:T(8,128)} %conc.1) | copy-start | bytes 393220
  5.9 0.7 %copy-start.9 = (f32[2]{0:T(128)S(1)}, f32[2]{0:T(128)}, u32[]{:S(2)}) copy-start(f32[2]{0:T(128)} %settle.1) | copy-start | bytes 28
  5.9 0.7 %copy-start.10 = (f32[2]{0:T(128)S(1)}, f32[2]{0:T(128)}, u32[]{:S(2)}) copy-start(f32[2]{0:T(128)} %critical.1) | copy-start | bytes 28
  5.9 0.7 %copy-start.11 = (f32[2]{0:T(128)S(1)}, f32[2]{0:T(128)}, u32[]{:S(2)}) copy-start(f32[2]{0:T(128)} %erosion.1) | copy-start | bytes 28
  6.6 1.2 %copy-start = (bf16[64,64,64]{2,1,0:T(8,128)(2,1)S(1)}, bf16[64,64,64]{2,1,0:T(8,128)(2,1)}, u32[]{:S(2)}) copy-start(bf16[64,64,64]{2,1,0:T(8,128)(2,1)} %param.43) | copy-start | bytes 1572868
  7.8 0.8 %copy-start.3 = (s32[32,512]{1,0:T(8,128)S(1)}, s32[32,512]{1,0:T(8,128)}, u32[]{:S(2)}) copy-start(s32[32,512]{1,0:T(8,128)} %open_lo.1) | copy-start | bytes 196612
  8.7 0.8 %copy-start.4 = (s32[32,512]{1,0:T(8,128)S(1)}, s32[32,512]{1,0:T(8,128)}, u32[]{:S(2)}) copy-start(s32[32,512]{1,0:T(8,128)} %open_hi.1) | copy-start | bytes 196612
  9.5 0.8 %copy-start.5 = (s32[32,512]{1,0:T(8,128)S(1)}, s32[32,512]{1,0:T(8,128)}, u32[]{:S(2)}) copy-start(s32[32,512]{1,0:T(8,128)} %open_y.1) | copy-start | bytes 196612
  10.3 0.8 %copy-start.6 = (bf16[32,512]{1,0:T(8,128)(2,1)S(1)}, bf16[32,512]{1,0:T(8,128)(2,1)}, u32[]{:S(2)}) copy-start(bf16[32,512]{1,0:T(8,128)(2,1)} %flow_lo.1) | copy-start | bytes 98308
  11.1 0.8 %copy-start.7 = (bf16[32,512]{1,0:T(8,128)(2,1)S(1)}, bf16[32,512]{1,0:T(8,128)(2,1)}, u32[]{:S(2)}) copy-start(bf16[32,512]{1,0:T(8,128)(2,1)} %flow_hi.1) | copy-start | bytes 98308
  11.8 0.8 %copy-start.8 = (bf16[32,512]{1,0:T(8,128)(2,1)S(1)}, bf16[32,512]{1,0:T(8,128)(2,1)}, u32[]{:S(2)}) copy-start(bf16[32,512]{1,0:T(8,128)(2,1)} %flow_y.1) | copy-start | bytes 98308

commit v2 on v1

--- a/solution.py
+++ b/solution.py
@@ -15,6 +15,7 @@
 DRAG = 50.0
 TAU_CURRENT = 20.0
 TAU_WAVES = 10.0
+LOADS = 19
 MESH = pl.DeviceIdType.MESH
 F32 = jnp.float32
 BF16 = jnp.bfloat16
@@ -47,18 +48,35 @@
 
 def kernel(
     sizes,
-    conc, flow_lo, flow_hi, flow_y, open_lo, open_hi, open_y,
     settle, critical, erosion,
-    wave, bands, meta_in, ent_cols, ent_rows, weight,
-    sed_out, wave_out,
+    *refs,
+):
+    loads = len(refs[:LOADS])
+    sources, (sed_out, wave_out), local = refs[:loads], refs[loads : loads + 2], refs[loads + 2 :]
+    body(sizes, settle, critical, erosion, sources, sed_out, wave_out, local[:loads], *local[loads:])
+
+
+def body(
+    sizes, settle, critical, erosion, sources, sed_out, wave_out, targets,
     we, meta, conc_x, fields, tau_x, table, table_in, wf,
     select, inflow, keep, energy, split, orb, orb_in, gathered,
+    band_rows, ent_rows, load_sem,
     halo_send, halo_recv, table_send, table_recv, lev_send, lev_recv, orb_send, orb_recv,
 ):
     n_tile, n, n_lev = sizes
+    (
+        wave, neighbors, facing, live, flow_lo, flow_hi, flow_y, open_lo, open_hi, open_y,
+        owner, slot, cell, angle, speeds, growths, orbitals, weight, conc,
+    ) = targets
+    copies = [
+        pltpu.make_async_copy(source, target, load_sem.at[i])
+        for i, (source, target) in enumerate(zip(sources, targets))
+    ]
+    for copy in copies:
+        copy.start()
     bins = wave.shape[0]
     rows, cols = flow_lo.shape
-    ent = ent_cols.shape[0]
+    ent = cell.shape[0]
     pairs = 4 * n
     classes = conc.shape[0]
     sec, tile, lev = lax.axis_index("sec"), lax.axis_index("tile"), lax.axis_index("lev")
@@ -81,10 +99,107 @@
             barrier, inc=1, device_id={"lev": lax.rem(lev + off, n_lev)}, device_id_type=MESH
         )
 
+    for copy in copies[0:4]:
+        copy.wait()
+    toward = facing[...]
+    toward_c, toward_s = jnp.cos(toward), jnp.sin(toward)
+    near_f = neighbors[...].astype(F32)
+    live_f = live[...].astype(F32).reshape(1, live.shape[0])
     for j in range(4):
-        we[4 + j] = wave[:, 128 * j : 128 * j + 128].astype(F32)
-        meta[4 + j] = meta_in[:, 128 * j : 128 * j + 128]
-
+        lanes = slice(128 * j, 128 * j + 128)
+        we[4 + j] = wave[:, lanes].astype(F32)
+        meta[4 + j, 0:4, :] = near_f[:, lanes]
+        meta[4 + j, 4:8, :] = toward_c[:, lanes]
+        meta[4 + j, 8:12, :] = toward_s[:, lanes]
+        meta[4 + j, 12:16, :] = jnp.broadcast_to(live_f[:, lanes], (4, 128))
+
+    @pl.when(me == 0)
+    def _():
+        we[0:4] = jnp.zeros((4, bins, 128), F32)
+        meta[0:4] = jnp.zeros((4, 16, 128), F32)
+        fields[:, 0:8] = jnp.zeros((6, 8, cols), F32)
+        conc_x[:, 0:8] = jnp.zeros((classes, 8, cols), F32)
+        tau_x[0:8] = jnp.zeros((8, cols), F32)
+
+    @pl.when(me == n - 1)
+    def _():
+        we[8:12] = jnp.zeros((4, bins, 128), F32)
+        meta[8:12] = jnp.zeros((4, 16, 128), F32)
+        fields[:, rows + 8 : rows + 16] = jnp.zeros((6, 8, cols), F32)
+        conc_x[:, rows + 8 : rows + 16] = jnp.zeros((classes, 8, cols), F32)
+        tau_x[rows + 8 : rows + 16] = jnp.zeros((8, cols), F32)
+
+    pl.semaphore_wait(barrier, n - 1 + n_lev - 1)
+
+    def to_right(src, dst, i):
+        return pltpu.make_async_remote_copy(
+            src_ref=src, dst_ref=dst,
+            send_sem=halo_send.at[0, i], recv_sem=halo_recv.at[0, i],
+            device_id=plane(lax.rem(me + 1, n)), device_id_type=MESH,
+        )
+
+    def to_left(src, dst, i):
+        return pltpu.make_async_remote_copy(
+            src_ref=src, dst_ref=dst,
+            send_sem=halo_send.at[1, i], recv_sem=halo_recv.at[1, i],
+            device_id=plane(lax.rem(me + n - 1, n)), device_id_type=MESH,
+        )
+
+    own, before, after = pl.ds(4, 4), pl.ds(0, 4), pl.ds(8, 4)
+    top, bottom = pl.ds(8, 8), pl.ds(rows, 8)
+    above, below = pl.ds(0, 8), pl.ds(rows + 8, 8)
+    right = [
+        to_right(meta.at[own], meta.at[before], 0),
+        to_right(we.at[own], we.at[before], 1),
+        to_right(fields.at[:, bottom], fields.at[:, above], 2),
+        to_right(conc_x.at[:, bottom], conc_x.at[:, above], 3),
+        to_right(tau_x.at[bottom], tau_x.at[above], 4),
+    ]
+    left = [
+        to_left(meta.at[own], meta.at[after], 0),
+        to_left(we.at[own], we.at[after], 1),
+        to_left(fields.at[:, top], fields.at[:, below], 2),
+        to_left(conc_x.at[:, top], conc_x.at[:, below], 3),
+        to_left(tau_x.at[top], tau_x.at[below], 4),
+    ]
+
+    def start(items):
+        @pl.when(me < n - 1)
+        def _():
+            for i in items:
+                right[i].start()
+
+        @pl.when(me > 0)
+        def _():
+            for i in items:
+                left[i].start()
+
+    def arrived(items):
+        @pl.when(me > 0)
+        def _():
+            for i in items:
+                right[i].wait_recv()
+
+        @pl.when(me < n - 1)
+        def _():
+            for i in items:
+                left[i].wait_recv()
+
+    def sent(items):
+        @pl.when(me < n - 1)
+        def _():
+            for i in items:
+                right[i].wait_send()
+
+        @pl.when(me > 0)
+        def _():
+            for i in items:
+                left[i].wait_send()
+
+    start([0, 1])
+
+    for copy in copies[4:]:
+        copy.wait()
     lo, hi, side = flow_lo[...].astype(F32), flow_hi[...].astype(F32), flow_y[...].astype(F32)
     ol, oh, oy = open_lo[...].astype(F32), open_hi[...].astype(F32), open_y[...].astype(F32)
     first_col = iota((rows, cols), 1) == 0
@@ -112,91 +227,15 @@
     for c in range(classes):
         conc_x[c, mid] = conc[c]
 
-    @pl.when(me == 0)
-    def _():
-        we[0:4] = jnp.zeros((4, bins, 128), F32)
-        meta[0:4] = jnp.zeros((4, 16, 128), F32)
-        fields[:, 0:8] = jnp.zeros((6, 8, cols), F32)
-        conc_x[:, 0:8] = jnp.zeros((classes, 8, cols), F32)
-        tau_x[0:8] = jnp.zeros((8, cols), F32)
-
-    @pl.when(me == n - 1)
-    def _():
-        we[8:12] = jnp.zeros((4, bins, 128), F32)
-        meta[8:12] = jnp.zeros((4, 16, 128), F32)
-        fields[:, rows + 8 : rows + 16] = jnp.zeros((6, 8, cols), F32)
-        conc_x[:, rows + 8 : rows + 16] = jnp.zeros((classes, 8, cols), F32)
-        tau_x[rows + 8 : rows + 16] = jnp.zeros((8, cols), F32)
-
-    pl.semaphore_wait(barrier, n - 1 + n_lev - 1)
-
-    def to_right(src, dst, i):
-        return pltpu.make_async_remote_copy(
-            src_ref=src, dst_ref=dst,
-            send_sem=halo_send.at[0, i], recv_sem=halo_recv.at[0, i],
-            device_id=plane(lax.rem(me + 1, n)), device_id_type=MESH,
-        )
-
-    def to_left(src, dst, i):
-        return pltpu.make_async_remote_copy(
-            src_ref=src, dst_ref=dst,
-            send_sem=halo_send.at[1, i], recv_sem=halo_recv.at[1, i],
-            device_id=plane(lax.rem(me + n - 1, n)), device_id_type=MESH,
-        )
-
-    own, before, after = pl.ds(4, 4), pl.ds(0, 4), pl.ds(8, 4)
-    top, bottom = pl.ds(8, 8), pl.ds(rows, 8)
-    above, below = pl.ds(0, 8), pl.ds(rows + 8, 8)
-    right = [
-        to_right(meta.at[own], meta.at[before], 0),
-        to_right(we.at[own], we.at[before], 1),
-        to_right(fields.at[:, bottom], fields.at[:, above], 2),
-        to_right(conc_x.at[:, bottom], conc_x.at[:, above], 3),
-        to_right(tau_x.at[bottom], tau_x.at[above], 4),
-    ]
-    left = [
-        to_left(meta.at[own], meta.at[after], 0),
-        to_left(we.at[own], we.at[after], 1),
-        to_left(fields.at[:, top], fields.at[:, below], 2),
-        to_left(conc_x.at[:, top], conc_x.at[:, below], 3),
-        to_left(tau_x.at[top], tau_x.at[below], 4),
-    ]
-
-    def start(items):
-        @pl.when(me < n - 1)
-        def _():
-            for i in items:
-                right[i].start()
-
-        @pl.when(me > 0)
-        def _():
-            for i in items:
-                left[i].start()
-
-    def arrived(items):
-        @pl.when(me > 0)
-        def _():
-            for i in items:
-                right[i].wait_recv()
-
-        @pl.when(me < n - 1)
-        def _():
-            for i in items:
-                left[i].wait_recv()
-
-    def sent(items):
-        @pl.when(me < n - 1)
-        def _():
-            for i in items:
-                right[i].wait_send()
-
-        @pl.when(me > 0)
-        def _():
-            for i in items:
-                left[i].wait_send()
-
-    start([0, 1])
-
+
+    per_row = cols // 64
+    cells, slots = cell[...].reshape(1, ent), slot[...].reshape(1, ent)
+    pair_ids = owner[...].reshape(1, ent) * 4 + slots // 2
+    row_ids = cells // per_row
+    ent_rows[...] = jnp.zeros(ent_rows.shape, F32)
+    for i, x in enumerate([row_ids, cells % per_row, pair_ids, slots % 2]):
+        ent_rows[i : i + 1, 0:ent] = x.astype(F32)
+    ent_cols = ent_rows[...].T[0:ent].astype(jnp.int32)
     cell_row, cell_col = ent_cols[:, 0:1], ent_cols[:, 1:2]
     pair_col, parity = ent_cols[:, 2:3], ent_cols[:, 3:4]
     row_hot = (iota((ent, rows), 1) == cell_row).astype(F32).astype(BF16)
@@ -229,7 +268,7 @@
         ],
         axis=1,
     )
-    pair_hot = (iota((pairs, ent), 0) == ent_rows[0:1, :]).astype(F32).astype(BF16)
+    pair_hot = (iota((pairs, ent), 0) == pair_ids).astype(F32).astype(BF16)
     sums = dot(jnp.concatenate([pair_hot, pair_hot], axis=1), two(stacked, 0))
     table[0:4] = jnp.zeros((4, 4, 128), F32)
     table[pairs + 4 : pairs + 8] = jnp.zeros((4, 4, 128), F32)
@@ -260,7 +299,19 @@
             hot = (iota((384, 128), 0) == near[k : k + 1, :]).astype(F32)
             select[b, :, 128 * k : 128 * k + 128] = hot.astype(BF16)
 
-    arrived([1])
+    band_rows[...] = jnp.zeros(band_rows.shape, F32)
+    turn = angle[...].reshape(1, bins)
+    turn_c, turn_s = jnp.cos(turn), jnp.sin(turn)
+    gain_row = orbitals[...].reshape(1, bins)
+    for i, x in enumerate(
+        [
+            turn_c, turn_s, speeds[...].reshape(1, bins), growths[...].reshape(1, bins),
+            gain_row * turn_c, gain_row * turn_s,
+        ]
+    ):
+        band_rows[i : i + 1, 0:bins] = x
+    bands = band_rows[...].T[0:bins]
+
     wf[...] = table[pl.ds(4 * me, 12)]
 
     @pl.loop(1, n)
@@ -272,15 +323,11 @@
     pace, growth = bands[:, 2:3], bands[:, 3:4]
     coef_c, coef_s = bands[:, 4:5], bands[:, 5:6]
 
-    @pl.loop(0, 12)
+    @pl.loop(1, 11)
     def _(b):
         w = wf[b]
         m = meta[b]
         alive = m[12:13, :]
-        push = jnp.maximum(cosine * w[2:3, :] + sine * w[3:4, :], 0.0)
-        first = (we[b] + growth * push) * alive
-        energy[b] = first
-        split[0, b] = two(first, 0)
         drift = cosine * w[0:1, :] + sine * w[1:2, :]
         rate = pace * (0.5 + 0.25 * jnp.tanh(drift)) * alive
         total = jnp.zeros((bins, 128), F32)
@@ -291,6 +338,16 @@
             inflow[b, k] = flow
             total = total + flow
         keep[b] = alive - total
+
+    arrived([1])
+
+    @pl.loop(0, 12)
+    def _(b):
+        w = wf[b]
+        push = jnp.maximum(cosine * w[2:3, :] + sine * w[3:4, :], 0.0)
+        first = (we[b] + growth * push) * meta[b][12:13, :]
+        energy[b] = first
+        split[0, b] = two(first, 0)
 
     for step in range(WSTEPS):
         now, later = step % 2, (step + 1) % 2
@@ -369,7 +426,7 @@
         left_side = two(jnp.concatenate([x[8 * g : 8 * g + 8] for x in wide], axis=0), 0)
         block = dot(left_side, weight[512 * g : 512 * g + 512, :])
         spread.append(block[0:16] + block[16:32])
-    row_hot_t = (iota((rows, ent), 0) == ent_rows[1:2, :]).astype(F32).astype(BF16)
+    row_hot_t = (iota((rows, ent), 0) == row_ids).astype(F32).astype(BF16)
     placed = []
     for c in range(2):
         x = jnp.concatenate([y[8 * c : 8 * c + 8] for y in spread], axis=0)
@@ -424,30 +481,13 @@
     ent = remap_cell.shape[0]
     classes = ocean_conc.shape[0]
     pairs = 4 * n
-    per_row = cols // 64
-    cosine, sine = jnp.cos(band_angle), jnp.sin(band_angle)
-    nothing = jnp.zeros_like(cosine)
-    bands = jnp.stack(
-        [cosine, sine, band_speed, band_growth, band_orbital * cosine, band_orbital * sine,
-         nothing, nothing],
-        axis=1,
+    sources = (
+        wave_energy, neighbors, facing_angle, live_nodes,
+        flow_lo, flow_hi, flow_y, open_lo, open_hi, open_y,
+        remap_owner.reshape(ent), remap_slot, remap_cell,
+        band_angle, band_speed, band_growth, band_orbital,
+        remap_weight.reshape(ent * 64, 64), ocean_conc,
     )
-    meta = jnp.concatenate(
-        [
-            neighbors.astype(F32),
-            jnp.cos(facing_angle),
-            jnp.sin(facing_angle),
-            live_nodes.astype(F32)[None],
-            jnp.zeros((3, nodes), F32),
-        ],
-        axis=0,
-    )
-    owner = remap_owner[:, 0]
-    pair = owner * 4 + remap_slot // 2
-    ent_cols = jnp.stack(
-        [remap_cell // per_row, remap_cell % per_row, pair, remap_slot % 2], axis=1
-    )
-    ent_rows = jnp.stack([pair, remap_cell // per_row], axis=0)
     vmem = pl.BlockSpec(memory_space=pltpu.VMEM)
     smem = pl.BlockSpec(memory_space=pltpu.SMEM)
     tall = rows + 16
@@ -457,9 +497,10 @@
             jax.ShapeDtypeStruct(ocean_conc.shape, F32),
             jax.ShapeDtypeStruct(wave_energy.shape, BF16),
         ),
-        in_specs=[vmem] * 7 + [smem] * 3 + [vmem] * 6,
+        in_specs=[smem] * 3 + [pl.BlockSpec(memory_space=pl.ANY)] * LOADS,
         out_specs=(vmem, vmem),
-        scratch_shapes=[
+        scratch_shapes=[pltpu.VMEM(x.shape, x.dtype) for x in sources]
+        + [
             pltpu.VMEM((12, bins, 128), F32),
             pltpu.VMEM((12, 16, 128), F32),
             pltpu.VMEM((classes, tall, cols), F32),
@@ -476,6 +517,9 @@
             pltpu.VMEM((4, 2, 128), F32),
             pltpu.VMEM((n_lev, 4, 2, 128), F32),
             pltpu.VMEM((pairs, 2, 128), F32),
+            pltpu.VMEM((8, -(-bins // 128) * 128), F32),
+            pltpu.VMEM((8, -(-ent // 128) * 128), F32),
+            pltpu.SemaphoreType.DMA((LOADS,)),
             pltpu.SemaphoreType.DMA((2, 5)),
             pltpu.SemaphoreType.DMA((2, 5)),
             pltpu.SemaphoreType.DMA((n,)),
@@ -486,13 +530,9 @@
             pltpu.SemaphoreType.DMA((n,)),
         ],
         compiler_params=pltpu.CompilerParams(
-            collective_id=0, has_side_effects=True, vmem_limit_bytes=48 * 1024 * 1024
+            collective_id=0, has_side_effects=True, vmem_limit_bytes=56 * 1024 * 1024
         ),
-    )(
-        ocean_conc, flow_lo, flow_hi, flow_y, open_lo, open_hi, open_y,
-        settle_rate, critical_stress, erosion_rate,
-        wave_energy, bands, meta, ent_cols, ent_rows, remap_weight.reshape(ent * 64, 64),
-    )
+    )(settle_rate, critical_stress, erosion_rate, *sources)
 
 
 def solution(mesh):

time: 57.6 us -> 48.1 us (0.84)
  local copies, waits for them, and re-layouts: 10.4 us -> 2.29 us
  other arithmetic: 2.87 us -> 0 us
  Pallas kernels: 43 us -> 45 us
    unnamed x26 -> x4, local copies, waits for them, and re-layouts: 7.89 us -> 2.29 us
    pallas_call x1, Pallas kernels: 43 us -> 45 us  [per_device(): pl.pallas_call(functools.partial(kernel, (n_tile, n, n_lev)), out_shape=(...]
    sin x2 -> x0, local copies, waits for them, and re-layouts: 1.49 us -> none  [the longest x1 0.77 us: per_device(): jnp.sin(facing_angle)]
    convert_element_type x2 -> x0, other arithmetic: 1.46 us -> none  [the longest x1 0.74 us: per_device(): neighbors.astype(F32)]
    another operation x4 -> x0, local copies, waits for them, and re-layouts: 0.92 us -> none  [the longest x3 0.82 us: per_device(): jnp.stack([cosine, sine, band_speed, band_growth, band_orbital * cosine,...]
    select_n x1 -> x0, other arithmetic: 0.7 us -> none  [per_device(): remap_cell // per_row]
    mul x1 -> x0, other arithmetic: 0.69 us -> none  [per_device(): band_orbital * sine]
where the time goes in v2:
time: 48.1 us; the launch traced here: 48 us
  Pallas kernels  45 us (94%)
  local copies, waits for them, and re-layouts  2.29 us (5%)
  between operations  0.66 us (1%)
    pallas_call x1, Pallas kernels, per_device(): pl.pallas_call(functools.partial(kernel, (n_tile, n, n_lev)), out_shape=(...  45 us
    unnamed x4, local copies, waits for them, and re-layouts  2.29 us

profile of v2, /device:TPU:3, one launch (start us, length us, event | category | flops | bytes accessed | tf_op | source)
XLA Modules:
  0.0 48.0 jit_solution(2433417135053711465)
XLA Ops:
  0.6 45.0 %shard_map.221 = (f32[2,32,512]{2,1,0:T(8,128)}, bf16[192,512]{1,0:T(8,128)(2,1)}) custom-call(f32[2]{0:T(128)} %settle.1, f32[2]{0:T(128)} %critical.1, f32[2]{0:T(128)} %erosion.1, bf16[192,512]{1,0:T(8,128)(2,1)} %refs_0_.1, s32[4,512]{1,0:T(4,128)} %refs_1_.1, f32[4,512]{1,0:T(4,128)} %refs_2_.1, s32[512]{0:T(512)} %refs_3_.1, bf16[32,512]{1,0:T(8,128)(2,1)} %refs_4_.1, ...), custom_call_target="tpu_custom_call" | custom-call | tf_op jit(solution)/shard_map/pallas_call | solution.py:494
  45.7 0.0 copy-start
  45.7 1.6 %copy.26 = f32[2,32,512]{2,1,0:T(8,128)} copy(f32[2,32,512]{2,1,0:T(8,128)} %get-tuple-element.4) | data formatting | bytes 262144
  47.3 0.0 copy-done
  47.3 0.7 %copy.27 = bf16[192,512]{1,0:T(8,128)(2,1)} copy(bf16[192,512]{1,0:T(8,128)(2,1)S(1)} %copy-done) | data formatting | bytes 393216
Async XLA Ops:
  45.7 1.6 %copy-start = (bf16[192,512]{1,0:T(8,128)(2,1)S(1)}, bf16[192,512]{1,0:T(8,128)(2,1)}, u32[]{:S(2)}) copy-start(bf16[192,512]{1,0:T(8,128)(2,1)} %get-tuple-element.5) | copy-start | bytes 589828

commit v3 on v2

--- a/solution.py
+++ b/solution.py
@@ -60,7 +60,7 @@
     sizes, settle, critical, erosion, sources, sed_out, wave_out, targets,
     we, meta, conc_x, fields, tau_x, table, table_in, wf,
     select, inflow, keep, energy, split, orb, orb_in, gathered,
-    band_rows, ent_rows, load_sem,
+    band_rows, ent_rows, spread_bands, load_sem,
     halo_send, halo_recv, table_send, table_recv, lev_send, lev_recv, orb_send, orb_recv,
 ):
     n_tile, n, n_lev = sizes
@@ -207,26 +207,11 @@
     def left_of(x):
         return jnp.where(first_col, 0.0, pltpu.roll(x, 1, axis=1))
 
+    mid = pl.ds(8, rows)
     east = 0.5 * (lo + hi)
     north = 0.5 * (side + left_of(side))
     square = east * east + north * north
     speed = jnp.sqrt(square)
-    a_y = jnp.maximum(side, 0.0) + KAPPA * oy
-    b_y = jnp.minimum(side, 0.0) - KAPPA * oy
-    a_hi = jnp.maximum(hi, 0.0) + KAPPA * oh
-    b_hi = jnp.minimum(hi, 0.0) - KAPPA * oh
-    a_lo = jnp.maximum(lo, 0.0) + KAPPA * ol
-    b_lo = jnp.minimum(lo, 0.0) - KAPPA * ol
-    mid = pl.ds(8, rows)
-    fields[0, mid] = 1.0 - a_hi + b_lo - a_y + left_of(b_y)
-    fields[1, mid] = a_lo
-    fields[2, mid] = -b_hi
-    fields[3, mid] = -b_y
-    fields[4, mid] = left_of(a_y)
-    fields[5, mid] = TAU_CURRENT * square
-    for c in range(classes):
-        conc_x[c, mid] = conc[c]
-
 
     per_row = cols // 64
     cells, slots = cell[...].reshape(1, ent), slot[...].reshape(1, ent)
@@ -287,6 +272,21 @@
     def _(off):
         table_copy(off).start()
 
+
+    a_y = jnp.maximum(side, 0.0) + KAPPA * oy
+    b_y = jnp.minimum(side, 0.0) - KAPPA * oy
+    a_hi = jnp.maximum(hi, 0.0) + KAPPA * oh
+    b_hi = jnp.minimum(hi, 0.0) - KAPPA * oh
+    a_lo = jnp.maximum(lo, 0.0) + KAPPA * ol
+    b_lo = jnp.minimum(lo, 0.0) - KAPPA * ol
+    fields[0, mid] = 1.0 - a_hi + b_lo - a_y + left_of(b_y)
+    fields[1, mid] = a_lo
+    fields[2, mid] = -b_hi
+    fields[3, mid] = -b_y
+    fields[4, mid] = left_of(a_y)
+    fields[5, mid] = TAU_CURRENT * square
+    for c in range(classes):
+        conc_x[c, mid] = conc[c]
     start([2, 3])
 
     arrived([0])
@@ -311,6 +311,8 @@
     ):
         band_rows[i : i + 1, 0:bins] = x
     bands = band_rows[...].T[0:bins]
+    for i in range(6):
+        spread_bands[i] = jnp.broadcast_to(bands[:, i : i + 1], (bins, 128))
 
     wf[...] = table[pl.ds(4 * me, 12)]
 
@@ -319,12 +321,9 @@
         table_copy(off).wait_recv()
         wf[...] += table_in[off]
 
-    cosine, sine = bands[:, 0:1], bands[:, 1:2]
-    pace, growth = bands[:, 2:3], bands[:, 3:4]
-    coef_c, coef_s = bands[:, 4:5], bands[:, 5:6]
-
-    @pl.loop(1, 11)
+    @pl.loop(1, 11, unroll=2)
     def _(b):
+        cosine, sine, pace = spread_bands[0], spread_bands[1], spread_bands[2]
         w = wf[b]
         m = meta[b]
         alive = m[12:13, :]
@@ -341,8 +340,9 @@
 
     arrived([1])
 
-    @pl.loop(0, 12)
+    @pl.loop(0, 12, unroll=2)
     def _(b):
+        cosine, sine, growth = spread_bands[0], spread_bands[1], spread_bands[3]
         w = wf[b]
         push = jnp.maximum(cosine * w[2:3, :] + sine * w[3:4, :], 0.0)
         first = (we[b] + growth * push) * meta[b][12:13, :]
@@ -352,7 +352,7 @@
     for step in range(WSTEPS):
         now, later = step % 2, (step + 1) % 2
 
-        @pl.loop(step + 1, 11 - step)
+        @pl.loop(step + 1, 11 - step, unroll=2)
         def _(b):
             window = jnp.concatenate(
                 [split[now, b - 1], split[now, b], split[now, b + 1]], axis=1
@@ -368,8 +368,8 @@
 
     for j in range(4):
         final = energy[4 + j]
-        orb[j, 0:1, :] = jnp.sum(coef_c * final, axis=0, keepdims=True)
-        orb[j, 1:2, :] = jnp.sum(coef_s * final, axis=0, keepdims=True)
+        orb[j, 0:1, :] = jnp.sum(spread_bands[4] * final, axis=0, keepdims=True)
+        orb[j, 1:2, :] = jnp.sum(spread_bands[5] * final, axis=0, keepdims=True)
 
     def lev_copy(off):
         return pltpu.make_async_remote_copy(
@@ -519,6 +519,7 @@
             pltpu.VMEM((pairs, 2, 128), F32),
             pltpu.VMEM((8, -(-bins // 128) * 128), F32),
             pltpu.VMEM((8, -(-ent // 128) * 128), F32),
+            pltpu.VMEM((6, bins, 128), F32),
             pltpu.SemaphoreType.DMA((LOADS,)),
             pltpu.SemaphoreType.DMA((2, 5)),
             pltpu.SemaphoreType.DMA((2, 5)),

time: 48.1 us -> 43.4 us (0.902)
  Pallas kernels: 45 us -> 40.3 us
    pallas_call x1, Pallas kernels: 45 us -> 40.3 us  [per_device(): pl.pallas_call(functools.partial(kernel, (n_tile, n, n_lev)), out_shape=(...]
where the time goes in v3:
time: 43.4 us; the launch traced here: 43.3 us
  Pallas kernels  40.3 us (93%)
  local copies, waits for them, and re-layouts  2.29 us (5%)
  between operations  0.66 us (2%)
    pallas_call x1, Pallas kernels, per_device(): pl.pallas_call(functools.partial(kernel, (n_tile, n, n_lev)), out_shape=(...  40.3 us
    unnamed x4, local copies, waits for them, and re-layouts  2.29 us

profile of v3, /device:TPU:3, one launch (start us, length us, event | category | flops | bytes accessed | tf_op | source)
XLA Modules:
  0.0 43.3 jit_solution(7148420114568016774)
XLA Ops:
  0.6 40.3 %shard_map.221 = (f32[2,32,512]{2,1,0:T(8,128)}, bf16[192,512]{1,0:T(8,128)(2,1)}) custom-call(f32[2]{0:T(128)} %settle.1, f32[2]{0:T(128)} %critical.1, f32[2]{0:T(128)} %erosion.1, bf16[192,512]{1,0:T(8,128)(2,1)} %refs_0_.1, s32[4,512]{1,0:T(4,128)} %refs_1_.1, f32[4,512]{1,0:T(4,128)} %refs_2_.1, s32[512]{0:T(512)} %refs_3_.1, bf16[32,512]{1,0:T(8,128)(2,1)} %refs_4_.1, ...), custom_call_target="tpu_custom_call" | custom-call | tf_op jit(solution)/shard_map/pallas_call | solution.py:494
  41.0 0.0 copy-start
  41.0 1.6 %copy.26 = f32[2,32,512]{2,1,0:T(8,128)} copy(f32[2,32,512]{2,1,0:T(8,128)} %get-tuple-element.4) | data formatting | bytes 262144
  42.6 0.0 copy-done
  42.6 0.7 %copy.27 = bf16[192,512]{1,0:T(8,128)(2,1)} copy(bf16[192,512]{1,0:T(8,128)(2,1)S(1)} %copy-done) | data formatting | bytes 393216
Async XLA Ops:
  41.0 1.6 %copy-start = (bf16[192,512]{1,0:T(8,128)(2,1)S(1)}, bf16[192,512]{1,0:T(8,128)(2,1)}, u32[]{:S(2)}) copy-start(bf16[192,512]{1,0:T(8,128)(2,1)} %get-tuple-element.5) | copy-start | bytes 589828

commit v4 on v3

--- a/solution.py
+++ b/solution.py
@@ -291,7 +291,7 @@
 
     arrived([0])
 
-    @pl.loop(1, 11)
+    @pl.loop(1, 11, unroll=2)
     def _(b):
         base = (4 * me - 5 + b) * 128
         near = meta[b][0:NBRS].astype(jnp.int32) - base
@@ -352,7 +352,7 @@
     for step in range(WSTEPS):
         now, later = step % 2, (step + 1) % 2
 
-        @pl.loop(step + 1, 11 - step, unroll=2)
+        @pl.loop(step + 1, 11 - step, unroll=5 - step)
         def _(b):
             window = jnp.concatenate(
                 [split[now, b - 1], split[now, b], split[now, b + 1]], axis=1

time: 43.4 us -> 42.4 us (0.977)
  Pallas kernels: 40.3 us -> 39.3 us
    pallas_call x1, Pallas kernels: 40.3 us -> 39.3 us  [per_device(): pl.pallas_call(functools.partial(kernel, (n_tile, n, n_lev)), out_shape=(...]
where the time goes in v4:
time: 42.4 us; the launch traced here: 42.2 us
  Pallas kernels  39.3 us (93%)
  local copies, waits for them, and re-layouts  2.29 us (5%)
  between operations  0.66 us (2%)
    pallas_call x1, Pallas kernels, per_device(): pl.pallas_call(functools.partial(kernel, (n_tile, n, n_lev)), out_shape=(...  39.3 us
    unnamed x4, local copies, waits for them, and re-layouts  2.29 us

profile of v4, /device:TPU:3, one launch (start us, length us, event | category | flops | bytes accessed | tf_op | source)
XLA Modules:
  0.0 42.2 jit_solution(6054062667108473200)
XLA Ops:
  0.6 39.3 %shard_map.221 = (f32[2,32,512]{2,1,0:T(8,128)}, bf16[192,512]{1,0:T(8,128)(2,1)}) custom-call(f32[2]{0:T(128)} %settle.1, f32[2]{0:T(128)} %critical.1, f32[2]{0:T(128)} %erosion.1, bf16[192,512]{1,0:T(8,128)(2,1)} %refs_0_.1, s32[4,512]{1,0:T(4,128)} %refs_1_.1, f32[4,512]{1,0:T(4,128)} %refs_2_.1, s32[512]{0:T(512)} %refs_3_.1, bf16[32,512]{1,0:T(8,128)(2,1)} %refs_4_.1, ...), custom_call_target="tpu_custom_call" | custom-call | tf_op jit(solution)/shard_map/pallas_call | solution.py:494
  39.9 0.0 copy-start
  39.9 1.6 %copy.26 = f32[2,32,512]{2,1,0:T(8,128)} copy(f32[2,32,512]{2,1,0:T(8,128)} %get-tuple-element.4) | data formatting | bytes 262144
  41.5 0.0 copy-done
  41.5 0.7 %copy.27 = bf16[192,512]{1,0:T(8,128)(2,1)} copy(bf16[192,512]{1,0:T(8,128)(2,1)S(1)} %copy-done) | data formatting | bytes 393216
Async XLA Ops:
  39.9 1.6 %copy-start = (bf16[192,512]{1,0:T(8,128)(2,1)S(1)}, bf16[192,512]{1,0:T(8,128)(2,1)}, u32[]{:S(2)}) copy-start(bf16[192,512]{1,0:T(8,128)(2,1)} %get-tuple-element.5) | copy-start | bytes 589828
